TPU v7x, 32 devices: a whole 2x2x4 slice. The times are simulated.
32 devices in a mesh: seq: 8 (over y, x, core), head: 4 (over z).
Axes of the slice: x: 2, y: 2, z: 4, core: 2. Of those that a mesh axis runs over, the one named last changes fastest.
Arguments:
- queries: bfloat16 [9216, 5120], P(('seq', 'head')), may hold values from -120 to 120
- key_vectors: bfloat16 [9216, 5120], P(('seq', 'head')), may hold values from -20 to 20
- value_vectors: bfloat16 [9216, 5120], P(('seq', 'head')), may hold values from -6 to 6
- reach_time: int32 [24], P('seq'), may hold values from 0 to 1
- reach_width: int32 [24], P('seq'), may hold values from 0 to 2
- keep_mask: int32 [9216, 40], P('seq', 'head'), may hold values 0 or 1
Outputs:
- attended: bfloat16 [9216, 5120], P(('seq', 'head'))
All inputs are finite; a program needn't handle non-finite values. No bound on the sum of `keep_mask` on one device may be relied on, other than what follows from the above.
Results may differ from a plain program's by a relative error of at most 0.0046.
Values may be sent and summed in bfloat16 or wider, within the bound.
No kernel may reach another device: no remote copies, remote signals or barrier semaphores. Data moves between devices by JAX's collectives and lax.ppermute only.
A program may use at most 128 MiB of HBM per device.

v0:
```python
import functools
import math

import jax
import jax.numpy as jnp
from jax import lax
from jax.experimental import pallas as pl
from jax.experimental.pallas import tpu as pltpu
from jax.sharding import PartitionSpec as P

LANES = 128
CHUNKS = 4
ANY = pl.BlockSpec(memory_space=pl.ANY)
VMEM_LIMIT = 56 * 2**20


def tile_mask(reach_t, reach_w, slab_index, slab_count):
    tile_count = reach_t.shape[0]
    places = jnp.arange(tile_count, dtype=jnp.int32)
    columns = jnp.arange(3 * tile_count, dtype=jnp.int32)
    offsets = columns // tile_count - 1
    key_place = columns % tile_count
    inside = (slab_index + offsets >= 0) & (slab_index + offsets < slab_count)
    near_time = jnp.abs(offsets)[None, :] <= reach_t[:, None]
    near_width = jnp.abs(key_place[None, :] - places[:, None]) <= reach_w[:, None]
    return near_time & near_width & inside[None, :]


def run_copies(sems, pairs):
    copies = [
        pltpu.make_async_copy(source, target, sems.at[i]) for i, (source, target) in enumerate(pairs)
    ]
    for copy in copies:
        copy.start()
    for copy in copies:
        copy.wait()


def pack(arrays, after, groups, group_width, start, width):
    rows = arrays[0].shape[0]

    def kernel(*refs):
        sources, outs, sems = refs[:3], refs[3 + len(after) : -1], refs[-1]
        me = lax.axis_index("head")
        pairs = []
        for shift in range(groups):
            group = lax.rem(me + shift, groups)
            column = pl.multiple_of(group * group_width + start, LANES)
            for i, source in enumerate(sources):
                pairs.append(
                    (source.at[:, pl.ds(column, width)], outs[shift].at[:, pl.ds(i * width, width)])
                )
        run_copies(sems, pairs)

    return pl.pallas_call(
        kernel,
        in_specs=[ANY] * (3 + len(after)),
        out_specs=[ANY] * groups,
        out_shape=[jax.ShapeDtypeStruct((rows, 3 * width), jnp.bfloat16)] * groups,
        scratch_shapes=[pltpu.SemaphoreType.DMA((3 * groups,))],
        cost_estimate=pl.CostEstimate(
            flops=0, bytes_accessed=12 * groups * rows * width, transcendentals=0
        ),
        compiler_params=pltpu.CompilerParams(vmem_limit_bytes=VMEM_LIMIT),
        name="pack",
    )(*arrays, *after)


def assemble(pieces, after, width):
    groups = len(pieces)
    rows = pieces[0].shape[0]

    def kernel(*refs):
        parts, out, sems = refs[:groups], refs[-2], refs[-1]
        me = lax.axis_index("head")
        pairs = []
        for shift in range(groups):
            owner = lax.rem(me + groups - shift, groups)
            row = pl.multiple_of(owner * rows, 16)
            pairs.append((parts[shift].at[:, pl.ds(0, 2 * width)], out.at[pl.ds(row, rows), :]))
        run_copies(sems, pairs)

    return pl.pallas_call(
        kernel,
        in_specs=[ANY] * (groups + len(after)),
        out_specs=ANY,
        out_shape=jax.ShapeDtypeStruct((groups * rows, 2 * width), jnp.bfloat16),
        scratch_shapes=[pltpu.SemaphoreType.DMA((groups,))],
        cost_estimate=pl.CostEstimate(
            flops=0, bytes_accessed=8 * groups * rows * width, transcendentals=0
        ),
        compiler_params=pltpu.CompilerParams(vmem_limit_bytes=VMEM_LIMIT),
        name="assemble",
    )(*pieces, *after)


def place(chunks, group_width, total_width, target=None):
    groups = len(chunks[0][1])
    rows = chunks[0][1][0].shape[0]
    blocks = [block for _, parts in chunks for block in parts]
    extra = [] if target is None else [target]

    def kernel(*refs):
        out, sems = refs[-2], refs[-1]
        me = lax.axis_index("head")
        pairs = []
        for i, (start, parts) in enumerate(chunks):
            for shift, part in enumerate(parts):
                group = lax.rem(me + shift, groups)
                column = pl.multiple_of(group * group_width + start, LANES)
                pairs.append((refs[i * groups + shift], out.at[:, pl.ds(column, part.shape[1])]))
        run_copies(sems, pairs)

    return pl.pallas_call(
        kernel,
        in_specs=[ANY] * (len(blocks) + len(extra)),
        out_specs=ANY,
        out_shape=jax.ShapeDtypeStruct((rows, total_width), jnp.bfloat16),
        scratch_shapes=[pltpu.SemaphoreType.DMA((len(blocks),))],
        input_output_aliases={len(blocks): 0} if extra else {},
        cost_estimate=pl.CostEstimate(
            flops=0,
            bytes_accessed=4 * rows * sum(block.shape[1] for block in blocks),
            transcendentals=0,
        ),
        compiler_params=pltpu.CompilerParams(vmem_limit_bytes=VMEM_LIMIT),
        name="place",
    )(*blocks, *extra)


def lane_fold(op, wide):
    folded = wide[:, :LANES]
    for start in range(LANES, wide.shape[1], LANES):
        folded = op(folded, wide[:, start : start + LANES])
    return folded


def attend_kernel(groups, heads, first_head, tile_count, *refs):
    plan_ref, pieces = refs[0], refs[1 : 1 + groups]
    prev_ref, own_ref, next_ref, keep_ref = refs[1 + groups : 5 + groups]
    outs = refs[-6 - groups : -6]
    q_ref, out_ref, scores_ref, top_ref, total_ref, sum_ref = refs[-6:]
    slab_rows, width = q_ref.shape
    local_rows = slab_rows // groups
    head_size = width // heads
    tile_rows = slab_rows // tile_count
    scale = math.log2(math.e) / math.sqrt(head_size)
    slabs = ((0, prev_ref), (1, own_ref), (2, next_ref))
    me = lax.axis_index("head")

    def owner_rows(shift):
        owner = lax.rem(me + groups - shift, groups)
        return pl.ds(pl.multiple_of(owner * local_rows, 16), local_rows)

    def tile(index):
        return pl.ds(pl.multiple_of(index * tile_rows, tile_rows), tile_rows)

    def lanes(index):
        return pl.ds(index * head_size, head_size)

    for shift in range(groups):
        q_ref[owner_rows(shift), :] = pieces[shift][...]

    def one_tile(i, carry):
        top_ref[...] = jnp.full_like(top_ref, -jnp.inf)
        total_ref[...] = jnp.zeros_like(total_ref)
        sum_ref[...] = jnp.zeros_like(sum_ref)

        for slab, pair_ref in slabs:

            def score(place, carry, slab=slab, pair_ref=pair_ref):
                column = slab * tile_count + place

                @pl.when(plan_ref[i * 3 * tile_count + column] > 0)
                def _():
                    for h in range(heads):
                        found = lax.dot_general(
                            q_ref[tile(i), lanes(h)],
                            pair_ref[tile(place), lanes(h)],
                            (((1,), (1,)), ((), ())),
                            preferred_element_type=jnp.float32,
                        )
                        scores_ref[h, column] = found
                        top_ref[h] = jnp.maximum(top_ref[h], lane_fold(jnp.maximum, found))

                return carry

            lax.fori_loop(0, tile_count, score, 0)

        for h in range(heads):
            highest = jnp.max(top_ref[h], axis=1, keepdims=True) * scale
            top_ref[h] = jnp.broadcast_to(highest, top_ref.shape[1:])

        for slab, pair_ref in slabs:

            def weigh(place, carry, slab=slab, pair_ref=pair_ref):
                column = slab * tile_count + place

                @pl.when(plan_ref[i * 3 * tile_count + column] > 0)
                def _():
                    for h in range(heads):
                        highest = jnp.concatenate([top_ref[h]] * (tile_rows // LANES), axis=1)
                        weights = jnp.exp2(scores_ref[h, column] * scale - highest)
                        total_ref[h] += lane_fold(jnp.add, weights)
                        sum_ref[h] += jnp.dot(
                            weights.astype(jnp.bfloat16),
                            pair_ref[tile(place), lanes(heads + h)],
                            preferred_element_type=jnp.float32,
                        )

                return carry

            lax.fori_loop(0, tile_count, weigh, 0)

        keep = keep_ref[tile(i), :].astype(jnp.float32)
        numbers = lax.broadcasted_iota(jnp.int32, keep.shape, 1)
        for h in range(heads):
            totals = jnp.sum(total_ref[h], axis=1, keepdims=True)
            mine = jnp.where(numbers == first_head + h, keep, 0.0)
            factor = jnp.sum(mine, axis=1, keepdims=True) * (10.0 / 9.0)
            out_ref[tile(i), lanes(h)] = (sum_ref[h] * (factor / totals)).astype(out_ref.dtype)
        return carry

    lax.fori_loop(0, tile_count, one_tile, 0)

    for shift in range(groups):
        outs[shift][...] = out_ref[owner_rows(shift), :]


def attend(plan, pieces, prev, own, behind, keep_mask, after, first_head, heads, tile_count):
    groups = len(pieces)
    slab_rows = own.shape[0]
    local_rows = slab_rows // groups
    width = own.shape[1] // 2
    tile_rows = slab_rows // tile_count
    head_size = width // heads
    pairs = heads * slab_rows * 3 * slab_rows
    whole = pl.BlockSpec(own.shape, lambda s, plan: (0, 0))
    accumulator = pltpu.VMEM((heads, tile_rows, LANES), jnp.float32)
    return pl.pallas_call(
        functools.partial(attend_kernel, groups, heads, first_head, tile_count),
        grid_spec=pltpu.PrefetchScalarGridSpec(
            num_scalar_prefetch=1,
            grid=(1,),
            in_specs=[pl.BlockSpec((local_rows, width), lambda s, plan: (0, 2))] * groups
            + [whole] * 3
            + [pl.BlockSpec(keep_mask.shape, lambda s, plan: (0, 0))]
            + [ANY] * len(after),
            out_specs=[pl.BlockSpec((local_rows, width), lambda s, plan: (0, 0))] * groups,
            scratch_shapes=[
                pltpu.VMEM((slab_rows, width), jnp.bfloat16),
                pltpu.VMEM((slab_rows, width), jnp.bfloat16),
                pltpu.VMEM((heads, 3 * tile_count, tile_rows, tile_rows), jnp.float32),
                accumulator,
                accumulator,
                pltpu.VMEM((heads, tile_rows, head_size), jnp.float32),
            ],
        ),
        out_shape=[jax.ShapeDtypeStruct((local_rows, width), jnp.bfloat16)] * groups,
        compiler_params=pltpu.CompilerParams(vmem_limit_bytes=VMEM_LIMIT),
        cost_estimate=pl.CostEstimate(
            flops=16 * pairs * head_size,
            bytes_accessed=16 * slab_rows * width,
            transcendentals=pairs,
        ),
        name="attend",
    )(plan, *pieces, prev, own, behind, keep_mask, *after)


def on_device(queries, key_vectors, value_vectors, reach_time, reach_width, keep_mask):
    groups = lax.axis_size("head")
    slab_count = lax.axis_size("seq")
    total_width = queries.shape[1]
    group_heads = keep_mask.shape[1]
    group_width = total_width // groups
    head_size = group_width // group_heads
    tile_count = reach_time.shape[0]
    allowed = tile_mask(reach_time, reach_width, lax.axis_index("seq"), slab_count)
    plan = allowed.astype(jnp.int32).reshape(-1)
    onward = [(i, i + 1) for i in range(slab_count - 1)]
    backward = [(i + 1, i) for i in range(slab_count - 1)]

    def turn(array, shift):
        return lax.ppermute(array, "head", [(i, (i + shift) % groups) for i in range(groups)])

    count = min(CHUNKS, group_heads)
    sizes = [group_heads // count + (i < group_heads % count) for i in range(count)]
    firsts = [sum(sizes[:i]) for i in range(count)]
    sources = (key_vectors, value_vectors, queries)

    def send(i, after):
        width = sizes[i] * head_size
        blocks = pack(sources, after, groups, group_width, firsts[i] * head_size, width)
        return [blocks[0]] + [turn(blocks[shift], shift) for shift in range(1, groups)]

    pieces = [send(i, []) for i in range(min(2, count))]
    done = []
    for i, heads in enumerate(sizes):
        own = assemble(
            pieces[i],
            [part[0] for part in pieces[i + 1 :]] + [part[1][0] for part in done[-1:]],
            heads * head_size,
        )
        before = lax.ppermute(own, "seq", onward)
        behind = lax.ppermute(own, "seq", backward)
        if i + 2 < count:
            pieces.append(send(i + 2, [own]))
        hold = [part[0] for part in pieces[i + 2 :]]
        outs = attend(
            plan, pieces[i], before, own, behind, keep_mask, hold, firsts[i], heads, tile_count
        )
        back = [outs[0]] + [turn(outs[shift], groups - shift) for shift in range(1, groups)]
        done.append((firsts[i] * head_size, back))
    early = place(done[:-1], group_width, total_width) if count > 1 else None
    return place(done[-1:], group_width, total_width, early)


def solution(mesh):
    return jax.shard_map(
        on_device,
        mesh=mesh,
        in_specs=(
            P(("seq", "head"), None),
            P(("seq", "head"), None),
            P(("seq", "head"), None),
            P("seq"),
            P("seq"),
            P("seq", "head"),
        ),
        out_specs=P(("seq", "head"), None),
        check_vma=False,
    )
```

profile of v0, /device:TPU:2, one launch (start us, length us, event | category | flops | bytes accessed | tf_op | source)
XLA Modules:
  0.0 733.4 jit_solution(4084757822972030018)
XLA Ops:
  0.0 81.6 %pack.5 = (bf16[288,1152]{1,0:T(8,128)(2,1)}, bf16[288,1152]{1,0:T(8,128)(2,1)}, bf16[288,1152]{1,0:T(8,128)(2,1)}, bf16[288,1152]{1,0:T(8,128)(2,1)}) custom-call(bf16[288,5120]{1,0:T(8,128)(2,1)} %refs_0_.7, bf16[288,5120]{1,0:T(8,128)(2,1)} %refs_1_.7, bf16[288,5120]{1,0:T(8,128)(2,1)} %refs_2_.7), custom_call_target="tpu_custom_call" | custom-call | bytes 5308416 | tf_op jit(solution)/shard_map/pack/pallas_call | solution.py:55
  83.2 2.6 collective-permute-start.4
  87.2 81.6 %pack.4 = (bf16[288,1152]{1,0:T(8,128)(2,1)}, bf16[288,1152]{1,0:T(8,128)(2,1)}, bf16[288,1152]{1,0:T(8,128)(2,1)}, bf16[288,1152]{1,0:T(8,128)(2,1)}) custom-call(bf16[288,5120]{1,0:T(8,128)(2,1)} %refs_0_.7, bf16[288,5120]{1,0:T(8,128)(2,1)} %refs_1_.7, bf16[288,5120]{1,0:T(8,128)(2,1)} %refs_2_.7), custom_call_target="tpu_custom_call" | custom-call | bytes 5308416 | tf_op jit(solution)/shard_map/pack/pallas_call | solution.py:55
  170.2 54.7 %assemble.4.refs_3_.refs_6_ = bf16[1152,768]{1,0:T(8,128)(2,1)} custom-call(bf16[288,1152]{1,0:T(8,128)(2,1)} %get-tuple-element.41.refs_0_.refs_1_, bf16[288,1152]{1,0:T(8,128)(2,1)} %copy-done.3, bf16[288,1152]{1,0:T(8,128)(2,1)} %copy-done.4, bf16[288,1152]{1,0:T(8,128)(2,1)} %copy-done.5, bf16[288,1152]{1,0:T(8,128)(2,1)} %get-tuple-element.37.refs_4_.refs_0_.refs_1_), custom_call_target="tpu_custom_call" | custom-call | bytes 3538944 | tf_op jit(solution)/shard_map/assemble/pallas_call | solution.py:83
  224.9 1.9 collective-permute-start.7
  226.9 2.4 collective-permute-start.6
  230.3 2.8 collective-permute-start.2
  235.0 54.8 %pack.6 = (bf16[288,768]{1,0:T(8,128)(2,1)}, bf16[288,768]{1,0:T(8,128)(2,1)}, bf16[288,768]{1,0:T(8,128)(2,1)}, bf16[288,768]{1,0:T(8,128)(2,1)}) custom-call(bf16[288,5120]{1,0:T(8,128)(2,1)} %refs_0_.7, bf16[288,5120]{1,0:T(8,128)(2,1)} %refs_1_.7, bf16[288,5120]{1,0:T(8,128)(2,1)} %refs_2_.7, bf16[1152,768]{1,0:T(8,128)(2,1)} %assemble.4.refs_3_.refs_6_), custom_call_target="tpu_custom_call" | custom-call | bytes 3538944 | tf_op jit(solution)/shard_map/pack/pallas_call | solution.py:55
  289.8 15.9 %attend.4 = (bf16[288,384]{1,0:T(8,128)(2,1)}, bf16[288,384]{1,0:T(8,128)(2,1)}, bf16[288,384]{1,0:T(8,128)(2,1)}, bf16[288,384]{1,0:T(8,128)(2,1)}) custom-call(s32[27]{0:T(128)} %reshape.42.refs_0_, bf16[288,1152]{1,0:T(8,128)(2,1)} %get-tuple-element.41.refs_0_.refs_1_, bf16[288,1152]{1,0:T(8,128)(2,1)} %copy-done.3, bf16[288,1152]{1,0:T(8,128)(2,1)} %copy-done.4, ...), custom_call_target="tpu_custom_call" | custom-call | flops 24461180928 | bytes 7077888 | tf_op jit(solution)/shard_map/attend/pallas_call | solution.py:240
  307.1 54.7 %assemble.5.refs_3_.refs_6_ = bf16[1152,768]{1,0:T(8,128)(2,1)} custom-call(bf16[288,1152]{1,0:T(8,128)(2,1)} %get-tuple-element.37.refs_4_.refs_0_.refs_1_, bf16[288,1152]{1,0:T(8,128)(2,1)} %copy-done, bf16[288,1152]{1,0:T(8,128)(2,1)} %copy-done.1, bf16[288,1152]{1,0:T(8,128)(2,1)} %copy-done.2, ...), custom_call_target="tpu_custom_call" | custom-call | bytes 3538944 | tf_op jit(solution)/shard_map/assemble/pallas_call | solution.py:83
  361.8 9.2 %collective-permute-start.15 = (bf16[1152,768]{1,0:T(8,128)(2,1)}, bf16[1152,768]{1,0:T(8,128)(2,1)S(1)}, u32[]{:S(2)}, u32[]{:S(2)}) collective-permute-start(bf16[1152,768]{1,0:T(8,128)(2,1)} %assemble.5.refs_3_.refs_6_), channel_id=1, source_target_pairs={{4,0},{8,4},{12,8},{16,12},{20,16},{24,20},{28,24},{5,1},{9,5},{13... | collective-permute-start | bytes 5308424 | tf_op jit(solution)/shard_map/ppermute | solution.py:305
  374.8 2.8 collective-permute-start.13
  377.7 54.8 %pack.7 = (bf16[288,768]{1,0:T(8,128)(2,1)}, bf16[288,768]{1,0:T(8,128)(2,1)}, bf16[288,768]{1,0:T(8,128)(2,1)}, bf16[288,768]{1,0:T(8,128)(2,1)}) custom-call(bf16[288,5120]{1,0:T(8,128)(2,1)} %refs_0_.7, bf16[288,5120]{1,0:T(8,128)(2,1)} %refs_1_.7, bf16[288,5120]{1,0:T(8,128)(2,1)} %refs_2_.7, bf16[1152,768]{1,0:T(8,128)(2,1)} %assemble.5.refs_3_.refs_6_), custom_call_target="tpu_custom_call" | custom-call | bytes 3538944 | tf_op jit(solution)/shard_map/pack/pallas_call | solution.py:55
  434.3 15.9 %attend.5 = (bf16[288,384]{1,0:T(8,128)(2,1)}, bf16[288,384]{1,0:T(8,128)(2,1)}, bf16[288,384]{1,0:T(8,128)(2,1)}, bf16[288,384]{1,0:T(8,128)(2,1)}) custom-call(s32[27]{0:T(128)} %reshape.42.refs_0_, bf16[288,1152]{1,0:T(8,128)(2,1)} %get-tuple-element.37.refs_4_.refs_0_.refs_1_, bf16[288,1152]{1,0:T(8,128)(2,1)} %copy-done, bf16[288,1152]{1,0:T(8,128)(2,1)} %copy-done.1, ...), custom_call_target="tpu_custom_call" | custom-call | flops 24461180928 | bytes 7077888 | tf_op jit(solution)/shard_map/attend/pallas_call | solution.py:240
  451.3 36.9 %assemble.6.refs_6_ = bf16[1152,512]{1,0:T(8,128)(2,1)} custom-call(bf16[288,768]{1,0:T(8,128)(2,1)} %get-tuple-element.45.refs_9_.refs_4_.refs_0_.refs_1_, bf16[288,768]{1,0:T(8,128)(2,1)} %copy-done.9, bf16[288,768]{1,0:T(8,128)(2,1)} %copy-done.10, bf16[288,768]{1,0:T(8,128)(2,1)} %copy-done.11, ...), custom_call_target="tpu_custom_call" | custom-call | bytes 2359296 | tf_op jit(solution)/shard_map/assemble/pallas_call | solution.py:83
  488.1 9.4 %collective-permute-start.17 = (bf16[1152,512]{1,0:T(8,128)(2,1)}, bf16[1152,512]{1,0:T(8,128)(2,1)S(1)}, u32[]{:S(2)}, u32[]{:S(2)}) collective-permute-start(bf16[1152,512]{1,0:T(8,128)(2,1)} %assemble.6.refs_6_), channel_id=1, source_target_pairs={{4,0},{8,4},{12,8},{16,12},{20,16},{24,20},{28,24},{5,1},{9,5},{13... | collective-permute-start | bytes 3538952 | tf_op jit(solution)/shard_map/ppermute | solution.py:305
  500.9 2.8 collective-permute-start.10
  503.7 14.8 %collective-permute-done.17.refs_7_ = bf16[1152,512]{1,0:T(8,128)(2,1)S(1)} collective-permute-done((bf16[1152,512]{1,0:T(8,128)(2,1)}, bf16[1152,512]{1,0:T(8,128)(2,1)S(1)}, u32[]{:S(2)}, u32[]{:S(2)}) %collective-permute-start.17) | collective-permute-done | bytes 1179680 | tf_op jit(solution)/shard_map/ppermute | solution.py:305
  520.5 12.7 %attend.6 = (bf16[288,256]{1,0:T(8,128)(2,1)}, bf16[288,256]{1,0:T(8,128)(2,1)}, bf16[288,256]{1,0:T(8,128)(2,1)}, bf16[288,256]{1,0:T(8,128)(2,1)}) custom-call(s32[27]{0:T(128)} %reshape.42.refs_0_, bf16[288,768]{1,0:T(8,128)(2,1)} %get-tuple-element.45.refs_9_.refs_4_.refs_0_.refs_1_, bf16[288,768]{1,0:T(8,128)(2,1)} %copy-done.9, ...), custom_call_target="tpu_custom_call" | custom-call | flops 16307453952 | bytes 4718592 | tf_op jit(solution)/shard_map/attend/pallas_call | solution.py:240
  534.4 36.9 %assemble.7.refs_6_ = bf16[1152,512]{1,0:T(8,128)(2,1)} custom-call(bf16[288,768]{1,0:T(8,128)(2,1)} %get-tuple-element.47.refs_9_.refs_4_.refs_0_.refs_1_, bf16[288,768]{1,0:T(8,128)(2,1)} %copy-done.6, bf16[288,768]{1,0:T(8,128)(2,1)} %copy-done.7, bf16[288,768]{1,0:T(8,128)(2,1)} %copy-done.8, bf16[288,256]{1,0:T(8,128)(2,1)} %get-tuple-element.55.refs_4_.refs_8_), custom_call_target="tpu_custom_call" | custom-call | bytes 2359296 | tf_op jit(solution)/shard_map/assemble/pallas_call | solution.py:83
  571.3 9.1 %collective-permute-start.19 = (bf16[1152,512]{1,0:T(8,128)(2,1)}, bf16[1152,512]{1,0:T(8,128)(2,1)S(1)}, u32[]{:S(2)}, u32[]{:S(2)}) collective-permute-start(bf16[1152,512]{1,0:T(8,128)(2,1)} %assemble.7.refs_6_), channel_id=1, source_target_pairs={{4,0},{8,4},{12,8},{16,12},{20,16},{24,20},{28,24},{5,1},{9,5},{13... | collective-permute-start | bytes 3538952 | tf_op jit(solution)/shard_map/ppermute | solution.py:305
  582.3 2.5 collective-permute-start.23
  585.6 4.9 collective-permute-done.23.refs_1_
  590.5 3.5 collective-permute-start.26
  594.0 9.9 %collective-permute-done.24.refs_2_ = bf16[288,384]{1,0:T(8,128)(2,1)S(1)} collective-permute-done((bf16[288,384]{1,0:T(8,128)(2,1)S(1)}, bf16[288,384]{1,0:T(8,128)(2,1)S(1)}, u32[]{:S(2)}, u32[]{:S(2)}) %collective-permute-start.24) | collective-permute-done | bytes 221216 | tf_op jit(solution)/shard_map/ppermute | solution.py:284
  604.0 3.8 collective-permute-start.29
  607.9 12.7 %attend.7 = (bf16[288,256]{1,0:T(8,128)(2,1)}, bf16[288,256]{1,0:T(8,128)(2,1)}, bf16[288,256]{1,0:T(8,128)(2,1)}, bf16[288,256]{1,0:T(8,128)(2,1)}) custom-call(s32[27]{0:T(128)} %reshape.42.refs_0_, bf16[288,768]{1,0:T(8,128)(2,1)} %get-tuple-element.47.refs_9_.refs_4_.refs_0_.refs_1_, bf16[288,768]{1,0:T(8,128)(2,1)} %copy-done.6, ...), custom_call_target="tpu_custom_call" | custom-call | flops 16307453952 | bytes 4718592 | tf_op jit(solution)/shard_map/attend/pallas_call | solution.py:240
  622.2 7.7 %collective-permute-done.27.refs_6_ = bf16[288,384]{1,0:T(8,128)(2,1)S(1)} collective-permute-done((bf16[288,384]{1,0:T(8,128)(2,1)S(1)}, bf16[288,384]{1,0:T(8,128)(2,1)S(1)}, u32[]{:S(2)}, u32[]{:S(2)}) %collective-permute-start.27) | collective-permute-done | bytes 221216 | tf_op jit(solution)/shard_map/ppermute | solution.py:284
  630.9 2.7 collective-permute-start.22
  633.6 5.8 collective-permute-done.30.refs_10_
  640.7 72.7 %place.2.refs_4_ = bf16[288,5120]{1,0:T(8,128)(2,1)} custom-call(bf16[288,384]{1,0:T(8,128)(2,1)} %get-tuple-element.46.refs_5_.refs_0_, bf16[288,384]{1,0:T(8,128)(2,1)} %copy-done.12, bf16[288,384]{1,0:T(8,128)(2,1)} %copy-done.13, bf16[288,384]{1,0:T(8,128)(2,1)} %copy-done.14, bf16[288,384]{1,0:T(8,128)(2,1)} %get-tuple-element.54.refs_5_.refs_4_, ...), custom_call_target="tpu_custom_call" | custom-call | bytes 4718592 | tf_op jit(solution)/shard_map/place/pallas_call | solution.py:114
  714.2 19.0 %place.3 = bf16[288,5120]{1,0:T(8,128)(2,1)} custom-call(bf16[288,256]{1,0:T(8,128)(2,1)} %get-tuple-element.56.refs_0_, bf16[288,256]{1,0:T(8,128)(2,1)} %copy-done.18, bf16[288,256]{1,0:T(8,128)(2,1)} %copy-done.19, bf16[288,256]{1,0:T(8,128)(2,1)} %copy-done.20, bf16[288,5120]{1,0:T(8,128)(2,1)} %place.2.refs_4_), custom_call_target="tpu_custom_call", output_to_operand_aliasing={{}: (4, {})} | custom-call | bytes 1179648 | tf_op jit(solution)/shard_map/place/pallas_call | solution.py:114
  (147 shorter events, 29.1 us)
Async XLA Ops:
  81.6 87.2 %collective-permute-start.3 = (bf16[288,1152]{1,0:T(8,128)(2,1)}, bf16[288,1152]{1,0:T(8,128)(2,1)S(1)}, u32[]{:S(2)}, u32[]{:S(2)}) collective-permute-start(bf16[288,1152]{1,0:T(8,128)(2,1)} %get-tuple-element.42), channel_id=1, source_target_pairs={{0,1},{1,2},{2,3},{3,0},{4,5},{5,6},{6,7},{7,4},{8,9},{9,10},{10,1... | collective-permute-start | bytes 1990664 | tf_op jit(solution)/shard_map/ppermute | solution.py:284
  83.2 85.6 %collective-permute-start.4 = (bf16[288,1152]{1,0:T(8,128)(2,1)}, bf16[288,1152]{1,0:T(8,128)(2,1)S(1)}, u32[]{:S(2)}, u32[]{:S(2)}) collective-permute-start(bf16[288,1152]{1,0:T(8,128)(2,1)} %get-tuple-element.43), channel_id=1, source_target_pairs={{0,2},{1,3},{2,0},{3,1},{4,6},{5,7},{6,4},{7,5},{8,10},{9,11},{10,... | collective-permute-start | bytes 1990664 | tf_op jit(solution)/shard_map/ppermute | solution.py:284
  85.8 83.0 %collective-permute-start.5 = (bf16[288,1152]{1,0:T(8,128)(2,1)}, bf16[288,1152]{1,0:T(8,128)(2,1)S(1)}, u32[]{:S(2)}, u32[]{:S(2)}) collective-permute-start(bf16[288,1152]{1,0:T(8,128)(2,1)} %get-tuple-element.44), channel_id=1, source_target_pairs={{0,3},{1,0},{2,1},{3,2},{4,7},{5,4},{6,5},{7,6},{8,11},{9,8},{10,9... | collective-permute-start | bytes 1990664 | tf_op jit(solution)/shard_map/ppermute | solution.py:284
  224.9 64.8 %collective-permute-start.7 = (bf16[1152,768]{1,0:T(8,128)(2,1)}, bf16[1152,768]{1,0:T(8,128)(2,1)}, u32[]{:S(2)}, u32[]{:S(2)}) collective-permute-start(bf16[1152,768]{1,0:T(8,128)(2,1)} %assemble.4.refs_3_.refs_6_), channel_id=1, source_target_pairs={{4,0},{8,4},{12,8},{16,12},{20,16},{24,20},{28,24},{5,1},{9,5},{13... | collective-permute-start | bytes 5308424 | tf_op jit(solution)/shard_map/ppermute | solution.py:305
  226.9 62.9 %collective-permute-start.6 = (bf16[1152,768]{1,0:T(8,128)(2,1)}, bf16[1152,768]{1,0:T(8,128)(2,1)}, u32[]{:S(2)}, u32[]{:S(2)}) collective-permute-start(bf16[1152,768]{1,0:T(8,128)(2,1)} %assemble.4.refs_3_.refs_6_), channel_id=1, source_target_pairs={{0,4},{4,8},{8,12},{12,16},{16,20},{20,24},{24,28},{1,5},{5,9},{9,... | collective-permute-start | bytes 5308424 | tf_op jit(solution)/shard_map/ppermute | solution.py:304
  229.3 76.5 %collective-permute-start = (bf16[288,1152]{1,0:T(8,128)(2,1)}, bf16[288,1152]{1,0:T(8,128)(2,1)S(1)}, u32[]{:S(2)}, u32[]{:S(2)}) collective-permute-start(bf16[288,1152]{1,0:T(8,128)(2,1)} %get-tuple-element.38), channel_id=1, source_target_pairs={{0,1},{1,2},{2,3},{3,0},{4,5},{5,6},{6,7},{7,4},{8,9},{9,10},{10,1... | collective-permute-start | bytes 1990664 | tf_op jit(solution)/shard_map/ppermute | solution.py:284
  230.0 75.7 %collective-permute-start.1 = (bf16[288,1152]{1,0:T(8,128)(2,1)}, bf16[288,1152]{1,0:T(8,128)(2,1)S(1)}, u32[]{:S(2)}, u32[]{:S(2)}) collective-permute-start(bf16[288,1152]{1,0:T(8,128)(2,1)} %get-tuple-element.39), channel_id=1, source_target_pairs={{0,2},{1,3},{2,0},{3,1},{4,6},{5,7},{6,4},{7,5},{8,10},{9,11},{10,... | collective-permute-start | bytes 1990664 | tf_op jit(solution)/shard_map/ppermute | solution.py:284
  230.3 75.4 %collective-permute-start.2 = (bf16[288,1152]{1,0:T(8,128)(2,1)}, bf16[288,1152]{1,0:T(8,128)(2,1)S(1)}, u32[]{:S(2)}, u32[]{:S(2)}) collective-permute-start(bf16[288,1152]{1,0:T(8,128)(2,1)} %get-tuple-element.40), channel_id=1, source_target_pairs={{0,3},{1,0},{2,1},{3,2},{4,7},{5,4},{6,5},{7,6},{8,11},{9,8},{10,9... | collective-permute-start | bytes 1990664 | tf_op jit(solution)/shard_map/ppermute | solution.py:284
  361.8 70.7 %collective-permute-start.15 = (bf16[1152,768]{1,0:T(8,128)(2,1)}, bf16[1152,768]{1,0:T(8,128)(2,1)S(1)}, u32[]{:S(2)}, u32[]{:S(2)}) collective-permute-start(bf16[1152,768]{1,0:T(8,128)(2,1)} %assemble.5.refs_3_.refs_6_), channel_id=1, source_target_pairs={{4,0},{8,4},{12,8},{16,12},{20,16},{24,20},{28,24},{5,1},{9,5},{13... | collective-permute-start | bytes 5308424 | tf_op jit(solution)/shard_map/ppermute | solution.py:305
  371.0 61.5 %collective-permute-start.14 = (bf16[1152,768]{1,0:T(8,128)(2,1)}, bf16[1152,768]{1,0:T(8,128)(2,1)S(1)}, u32[]{:S(2)}, u32[]{:S(2)}) collective-permute-start(bf16[1152,768]{1,0:T(8,128)(2,1)} %assemble.5.refs_3_.refs_6_), channel_id=1, source_target_pairs={{0,4},{4,8},{8,12},{12,16},{16,20},{20,24},{24,28},{1,5},{5,9},{9,... | collective-permute-start | bytes 5308424 | tf_op jit(solution)/shard_map/ppermute | solution.py:304
  373.0 77.2 %collective-permute-start.11 = (bf16[288,768]{1,0:T(8,128)(2,1)S(1)}, bf16[288,768]{1,0:T(8,128)(2,1)S(1)}, u32[]{:S(2)}, u32[]{:S(2)}) collective-permute-start(bf16[288,768]{1,0:T(8,128)(2,1)S(1)} %copy-done.36), channel_id=1, source_target_pairs={{0,1},{1,2},{2,3},{3,0},{4,5},{5,6},{6,7},{7,4},{8,9},{9,10},{10,1... | collective-permute-start | bytes 1327112 | tf_op jit(solution)/shard_map/ppermute | solution.py:284
  373.6 76.6 %collective-permute-start.12 = (bf16[288,768]{1,0:T(8,128)(2,1)S(1)}, bf16[288,768]{1,0:T(8,128)(2,1)S(1)}, u32[]{:S(2)}, u32[]{:S(2)}) collective-permute-start(bf16[288,768]{1,0:T(8,128)(2,1)S(1)} %copy-done.34), channel_id=1, source_target_pairs={{0,2},{1,3},{2,0},{3,1},{4,6},{5,7},{6,4},{7,5},{8,10},{9,11},{10,... | collective-permute-start | bytes 1327112 | tf_op jit(solution)/shard_map/ppermute | solution.py:284
  374.8 75.4 %collective-permute-start.13 = (bf16[288,768]{1,0:T(8,128)(2,1)S(1)}, bf16[288,768]{1,0:T(8,128)(2,1)S(1)}, u32[]{:S(2)}, u32[]{:S(2)}) collective-permute-start(bf16[288,768]{1,0:T(8,128)(2,1)S(1)} %copy-done.33), channel_id=1, source_target_pairs={{0,3},{1,0},{2,1},{3,2},{4,7},{5,4},{6,5},{7,6},{8,11},{9,8},{10,9... | collective-permute-start | bytes 1327112 | tf_op jit(solution)/shard_map/ppermute | solution.py:284
  488.1 30.3 %collective-permute-start.17 = (bf16[1152,512]{1,0:T(8,128)(2,1)}, bf16[1152,512]{1,0:T(8,128)(2,1)S(1)}, u32[]{:S(2)}, u32[]{:S(2)}) collective-permute-start(bf16[1152,512]{1,0:T(8,128)(2,1)} %assemble.6.refs_6_), channel_id=1, source_target_pairs={{4,0},{8,4},{12,8},{16,12},{20,16},{24,20},{28,24},{5,1},{9,5},{13... | collective-permute-start | bytes 3538952 | tf_op jit(solution)/shard_map/ppermute | solution.py:305
  497.6 20.9 %collective-permute-start.16 = (bf16[1152,512]{1,0:T(8,128)(2,1)}, bf16[1152,512]{1,0:T(8,128)(2,1)S(1)}, u32[]{:S(2)}, u32[]{:S(2)}) collective-permute-start(bf16[1152,512]{1,0:T(8,128)(2,1)} %assemble.6.refs_6_), channel_id=1, source_target_pairs={{0,4},{4,8},{8,12},{12,16},{16,20},{20,24},{24,28},{1,5},{5,9},{9,... | collective-permute-start | bytes 3538952 | tf_op jit(solution)/shard_map/ppermute | solution.py:304
  499.5 33.7 %collective-permute-start.8 = (bf16[288,768]{1,0:T(8,128)(2,1)S(1)}, bf16[288,768]{1,0:T(8,128)(2,1)S(1)}, u32[]{:S(2)}, u32[]{:S(2)}) collective-permute-start(bf16[288,768]{1,0:T(8,128)(2,1)S(1)} %copy-done.38), channel_id=1, source_target_pairs={{0,1},{1,2},{2,3},{3,0},{4,5},{5,6},{6,7},{7,4},{8,9},{9,10},{10,1... | collective-permute-start | bytes 1327112 | tf_op jit(solution)/shard_map/ppermute | solution.py:284
  499.6 33.7 %collective-permute-start.9 = (bf16[288,768]{1,0:T(8,128)(2,1)S(1)}, bf16[288,768]{1,0:T(8,128)(2,1)S(1)}, u32[]{:S(2)}, u32[]{:S(2)}) collective-permute-start(bf16[288,768]{1,0:T(8,128)(2,1)S(1)} %copy-done.37), channel_id=1, source_target_pairs={{0,2},{1,3},{2,0},{3,1},{4,6},{5,7},{6,4},{7,5},{8,10},{9,11},{10,... | collective-permute-start | bytes 1327112 | tf_op jit(solution)/shard_map/ppermute | solution.py:284
  500.9 32.4 %collective-permute-start.10 = (bf16[288,768]{1,0:T(8,128)(2,1)S(1)}, bf16[288,768]{1,0:T(8,128)(2,1)S(1)}, u32[]{:S(2)}, u32[]{:S(2)}) collective-permute-start(bf16[288,768]{1,0:T(8,128)(2,1)S(1)} %copy-done.35), channel_id=1, source_target_pairs={{0,3},{1,0},{2,1},{3,2},{4,7},{5,4},{6,5},{7,6},{8,11},{9,8},{10,9... | collective-permute-start | bytes 1327112 | tf_op jit(solution)/shard_map/ppermute | solution.py:284
  571.3 32.6 %collective-permute-start.19 = (bf16[1152,512]{1,0:T(8,128)(2,1)}, bf16[1152,512]{1,0:T(8,128)(2,1)S(1)}, u32[]{:S(2)}, u32[]{:S(2)}) collective-permute-start(bf16[1152,512]{1,0:T(8,128)(2,1)} %assemble.7.refs_6_), channel_id=1, source_target_pairs={{4,0},{8,4},{12,8},{16,12},{20,16},{24,20},{28,24},{5,1},{9,5},{13... | collective-permute-start | bytes 3538952 | tf_op jit(solution)/shard_map/ppermute | solution.py:305
  580.4 23.6 %collective-permute-start.18 = (bf16[1152,512]{1,0:T(8,128)(2,1)}, bf16[1152,512]{1,0:T(8,128)(2,1)S(1)}, u32[]{:S(2)}, u32[]{:S(2)}) collective-permute-start(bf16[1152,512]{1,0:T(8,128)(2,1)} %assemble.7.refs_6_), channel_id=1, source_target_pairs={{0,4},{4,8},{8,12},{12,16},{16,20},{20,24},{24,28},{1,5},{5,9},{9,... | collective-permute-start | bytes 3538952 | tf_op jit(solution)/shard_map/ppermute | solution.py:304
  582.3 8.2 %collective-permute-start.23 = (bf16[288,384]{1,0:T(8,128)(2,1)S(1)}, bf16[288,384]{1,0:T(8,128)(2,1)S(1)}, u32[]{:S(2)}, u32[]{:S(2)}) collective-permute-start(bf16[288,384]{1,0:T(8,128)(2,1)S(1)} %copy-done.43), channel_id=1, source_target_pairs={{0,3},{1,0},{2,1},{3,2},{4,7},{5,4},{6,5},{7,6},{8,11},{9,8},{10,9... | collective-permute-start | bytes 663560 | tf_op jit(solution)/shard_map/ppermute | solution.py:284
  584.8 19.1 %collective-permute-start.24 = (bf16[288,384]{1,0:T(8,128)(2,1)S(1)}, bf16[288,384]{1,0:T(8,128)(2,1)S(1)}, u32[]{:S(2)}, u32[]{:S(2)}) collective-permute-start(bf16[288,384]{1,0:T(8,128)(2,1)S(1)} %copy-done.41), channel_id=1, source_target_pairs={{0,2},{1,3},{2,0},{3,1},{4,6},{5,7},{6,4},{7,5},{8,10},{9,11},{10,... | collective-permute-start | bytes 663560 | tf_op jit(solution)/shard_map/ppermute | solution.py:284
  585.6 35.0 %collective-permute-start.25 = (bf16[288,384]{1,0:T(8,128)(2,1)S(1)}, bf16[288,384]{1,0:T(8,128)(2,1)S(1)}, u32[]{:S(2)}, u32[]{:S(2)}) collective-permute-start(bf16[288,384]{1,0:T(8,128)(2,1)S(1)} %copy-done.39), channel_id=1, source_target_pairs={{0,1},{1,2},{2,3},{3,0},{4,5},{5,6},{6,7},{7,4},{8,9},{9,10},{10,1... | collective-permute-start | bytes 663560 | tf_op jit(solution)/shard_map/ppermute | solution.py:284
  590.5 31.2 %collective-permute-start.26 = (bf16[288,384]{1,0:T(8,128)(2,1)S(1)}, bf16[288,384]{1,0:T(8,128)(2,1)S(1)}, u32[]{:S(2)}, u32[]{:S(2)}) collective-permute-start(bf16[288,384]{1,0:T(8,128)(2,1)S(1)} %copy-done.44), channel_id=1, source_target_pairs={{0,3},{1,0},{2,1},{3,2},{4,7},{5,4},{6,5},{7,6},{8,11},{9,8},{10,9... | collective-permute-start | bytes 663560 | tf_op jit(solution)/shard_map/ppermute | solution.py:284
  603.9 26.0 %collective-permute-start.27 = (bf16[288,384]{1,0:T(8,128)(2,1)S(1)}, bf16[288,384]{1,0:T(8,128)(2,1)S(1)}, u32[]{:S(2)}, u32[]{:S(2)}) collective-permute-start(bf16[288,384]{1,0:T(8,128)(2,1)S(1)} %copy-done.42), channel_id=1, source_target_pairs={{0,2},{1,3},{2,0},{3,1},{4,6},{5,7},{6,4},{7,5},{8,10},{9,11},{10,... | collective-permute-start | bytes 663560 | tf_op jit(solution)/shard_map/ppermute | solution.py:284
  603.9 26.0 %collective-permute-start.28 = (bf16[288,384]{1,0:T(8,128)(2,1)S(1)}, bf16[288,384]{1,0:T(8,128)(2,1)S(1)}, u32[]{:S(2)}, u32[]{:S(2)}) collective-permute-start(bf16[288,384]{1,0:T(8,128)(2,1)S(1)} %copy-done.40), channel_id=1, source_target_pairs={{0,1},{1,2},{2,3},{3,0},{4,5},{5,6},{6,7},{7,4},{8,9},{9,10},{10,1... | collective-permute-start | bytes 663560 | tf_op jit(solution)/shard_map/ppermute | solution.py:284
  604.0 26.9 %collective-permute-start.29 = (bf16[288,256]{1,0:T(8,128)(2,1)S(1)}, bf16[288,256]{1,0:T(8,128)(2,1)S(1)}, u32[]{:S(2)}, u32[]{:S(2)}) collective-permute-start(bf16[288,256]{1,0:T(8,128)(2,1)S(1)} %copy-done.47), channel_id=1, source_target_pairs={{0,3},{1,0},{2,1},{3,2},{4,7},{5,4},{6,5},{7,6},{8,11},{9,8},{10,9... | collective-permute-start | bytes 442376 | tf_op jit(solution)/shard_map/ppermute | solution.py:284
  620.6 18.8 %collective-permute-start.30 = (bf16[288,256]{1,0:T(8,128)(2,1)S(1)}, bf16[288,256]{1,0:T(8,128)(2,1)S(1)}, u32[]{:S(2)}, u32[]{:S(2)}) collective-permute-start(bf16[288,256]{1,0:T(8,128)(2,1)S(1)} %copy-done.46), channel_id=1, source_target_pairs={{0,2},{1,3},{2,0},{3,1},{4,6},{5,7},{6,4},{7,5},{8,10},{9,11},{10,... | collective-permute-start | bytes 442376 | tf_op jit(solution)/shard_map/ppermute | solution.py:284
  621.7 17.7 %collective-permute-start.31 = (bf16[288,256]{1,0:T(8,128)(2,1)S(1)}, bf16[288,256]{1,0:T(8,128)(2,1)S(1)}, u32[]{:S(2)}, u32[]{:S(2)}) collective-permute-start(bf16[288,256]{1,0:T(8,128)(2,1)S(1)} %copy-done.45), channel_id=1, source_target_pairs={{0,1},{1,2},{2,3},{3,0},{4,5},{5,6},{6,7},{7,4},{8,9},{9,10},{10,1... | collective-permute-start | bytes 442376 | tf_op jit(solution)/shard_map/ppermute | solution.py:284
  629.9 83.5 %collective-permute-start.20 = (bf16[288,256]{1,0:T(8,128)(2,1)}, bf16[288,256]{1,0:T(8,128)(2,1)S(1)}, u32[]{:S(2)}, u32[]{:S(2)}) collective-permute-start(bf16[288,256]{1,0:T(8,128)(2,1)} %get-tuple-element.57), channel_id=1, source_target_pairs={{0,3},{1,0},{2,1},{3,2},{4,7},{5,4},{6,5},{7,6},{8,11},{9,8},{10,9... | collective-permute-start | bytes 442376 | tf_op jit(solution)/shard_map/ppermute | solution.py:284
  629.9 83.5 %collective-permute-start.21 = (bf16[288,256]{1,0:T(8,128)(2,1)}, bf16[288,256]{1,0:T(8,128)(2,1)S(1)}, u32[]{:S(2)}, u32[]{:S(2)}) collective-permute-start(bf16[288,256]{1,0:T(8,128)(2,1)} %get-tuple-element.58), channel_id=1, source_target_pairs={{0,2},{1,3},{2,0},{3,1},{4,6},{5,7},{6,4},{7,5},{8,10},{9,11},{10,... | collective-permute-start | bytes 442376 | tf_op jit(solution)/shard_map/ppermute | solution.py:284
  630.9 82.5 %collective-permute-start.22 = (bf16[288,256]{1,0:T(8,128)(2,1)}, bf16[288,256]{1,0:T(8,128)(2,1)S(1)}, u32[]{:S(2)}, u32[]{:S(2)}) collective-permute-start(bf16[288,256]{1,0:T(8,128)(2,1)} %get-tuple-element.59), channel_id=1, source_target_pairs={{0,1},{1,2},{2,3},{3,0},{4,5},{5,6},{6,7},{7,4},{8,9},{9,10},{10,1... | collective-permute-start | bytes 442376 | tf_op jit(solution)/shard_map/ppermute | solution.py:284
  (48 other events, 1132.4 us)
where the time goes:
time: 742 us; the launch traced here: 733 us
  Pallas kernels  605 us (82%)
  starting transfers between devices  72.2 us (10%)
  waiting for transfers between devices  43.1 us (6%)
  local copies, waits for them, and re-layouts  12.3 us (2%)
    pallas_call x4, Pallas kernels, pack(): pl.pallas_call(kernel, in_specs=[ANY] * (3 + len(after)), out_specs=[ANY]...  273 us
    pallas_call x4, Pallas kernels, assemble(): pl.pallas_call(kernel, in_specs=[ANY] * (groups + len(after)), out_specs=...  183 us
    pallas_call x2, Pallas kernels, place(): pl.pallas_call(kernel, in_specs=[ANY] * (len(blocks) + len(extra)), out_s...  91.7 us
    pallas_call x4, Pallas kernels, attend(): pl.pallas_call(functools.partial(attend_kernel, groups, heads, first_head...  57.1 us
    ppermute x24, starting transfers between devices, turn(): lax.ppermute(array, 'head', [(i, (i + shift) % groups) for i in range(gro...  34.3 us
    ppermute x4, starting transfers between devices, on_device(): behind = lax.ppermute(own, 'seq', backward)  29.7 us
    ppermute x24, waiting for transfers between devices, turn(): lax.ppermute(array, 'head', [(i, (i + shift) % groups) for i in range(gro...  28.3 us
  transfers between devices with their start and end apart: 32, of which 5 were waited for; matrix products, arithmetic and copies ran while one was open for 0% of the time, Pallas kernels for 44%

commit v1 on v0

--- a/solution.py
+++ b/solution.py
@@ -26,21 +26,32 @@
     return near_time & near_width & inside[None, :]
 
 
-def run_copies(sems, pairs):
-    copies = [
-        pltpu.make_async_copy(source, target, sems.at[i]) for i, (source, target) in enumerate(pairs)
+def staged(pairs, stages, sems):
+    arriving, leaving = [], []
+    for i, (source, target) in enumerate(pairs):
+        arriving.append(pltpu.make_async_copy(source, stages[i], sems.at[0, i]))
+        leaving.append(pltpu.make_async_copy(stages[i], target, sems.at[1, i]))
+    for copy in arriving:
+        copy.start()
+    for first, second in zip(arriving, leaving):
+        first.wait()
+        second.start()
+    for copy in leaving:
+        copy.wait()
+
+
+def stage_shapes(shapes):
+    return [pltpu.VMEM(shape, jnp.bfloat16) for shape in shapes] + [
+        pltpu.SemaphoreType.DMA((2, len(shapes)))
     ]
-    for copy in copies:
-        copy.start()
-    for copy in copies:
-        copy.wait()
 
 
 def pack(arrays, after, groups, group_width, start, width):
     rows = arrays[0].shape[0]
 
     def kernel(*refs):
-        sources, outs, sems = refs[:3], refs[3 + len(after) : -1], refs[-1]
+        sources, outs = refs[:3], refs[3 + len(after) : 3 + len(after) + groups]
+        stages, sems = refs[3 + len(after) + groups : -1], refs[-1]
         me = lax.axis_index("head")
         pairs = []
         for shift in range(groups):
@@ -50,14 +61,14 @@
                 pairs.append(
                     (source.at[:, pl.ds(column, width)], outs[shift].at[:, pl.ds(i * width, width)])
                 )
-        run_copies(sems, pairs)
+        staged(pairs, stages, sems)
 
     return pl.pallas_call(
         kernel,
         in_specs=[ANY] * (3 + len(after)),
         out_specs=[ANY] * groups,
         out_shape=[jax.ShapeDtypeStruct((rows, 3 * width), jnp.bfloat16)] * groups,
-        scratch_shapes=[pltpu.SemaphoreType.DMA((3 * groups,))],
+        scratch_shapes=stage_shapes([(rows, width)] * (3 * groups)),
         cost_estimate=pl.CostEstimate(
             flops=0, bytes_accessed=12 * groups * rows * width, transcendentals=0
         ),
@@ -71,21 +82,22 @@
     rows = pieces[0].shape[0]
 
     def kernel(*refs):
-        parts, out, sems = refs[:groups], refs[-2], refs[-1]
+        parts, out = refs[:groups], refs[groups + len(after)]
+        stages, sems = refs[groups + len(after) + 1 : -1], refs[-1]
         me = lax.axis_index("head")
         pairs = []
         for shift in range(groups):
             owner = lax.rem(me + groups - shift, groups)
             row = pl.multiple_of(owner * rows, 16)
             pairs.append((parts[shift].at[:, pl.ds(0, 2 * width)], out.at[pl.ds(row, rows), :]))
-        run_copies(sems, pairs)
+        staged(pairs, stages, sems)
 
     return pl.pallas_call(
         kernel,
         in_specs=[ANY] * (groups + len(after)),
         out_specs=ANY,
         out_shape=jax.ShapeDtypeStruct((groups * rows, 2 * width), jnp.bfloat16),
-        scratch_shapes=[pltpu.SemaphoreType.DMA((groups,))],
+        scratch_shapes=stage_shapes([(rows, 2 * width)] * groups),
         cost_estimate=pl.CostEstimate(
             flops=0, bytes_accessed=8 * groups * rows * width, transcendentals=0
         ),
@@ -101,7 +113,8 @@
     extra = [] if target is None else [target]
 
     def kernel(*refs):
-        out, sems = refs[-2], refs[-1]
+        out = refs[len(blocks) + len(extra)]
+        stages, sems = refs[len(blocks) + len(extra) + 1 : -1], refs[-1]
         me = lax.axis_index("head")
         pairs = []
         for i, (start, parts) in enumerate(chunks):
@@ -109,14 +122,14 @@
                 group = lax.rem(me + shift, groups)
                 column = pl.multiple_of(group * group_width + start, LANES)
                 pairs.append((refs[i * groups + shift], out.at[:, pl.ds(column, part.shape[1])]))
-        run_copies(sems, pairs)
+        staged(pairs, stages, sems)
 
     return pl.pallas_call(
         kernel,
         in_specs=[ANY] * (len(blocks) + len(extra)),
         out_specs=ANY,
         out_shape=jax.ShapeDtypeStruct((rows, total_width), jnp.bfloat16),
-        scratch_shapes=[pltpu.SemaphoreType.DMA((len(blocks),))],
+        scratch_shapes=stage_shapes([block.shape for block in blocks]),
         input_output_aliases={len(blocks): 0} if extra else {},
         cost_estimate=pl.CostEstimate(
             flops=0,

time: 742 us -> 333 us (0.45)
  the two profiles are of different devices: /device:TPU:2 before, /device:TPU:6 now
where the time goes in v1:
time: 333 us; the launch traced here: 328 us
  waiting for transfers between devices  109 us (33%)
  Pallas kernels  105 us (32%)
  starting transfers between devices  103 us (31%)
  local copies, waits for them, and re-layouts  10.4 us (3%)
    ppermute x24, starting transfers between devices, turn(): lax.ppermute(array, 'head', [(i, (i + shift) % groups) for i in range(gro...  83.9 us
    pallas_call x4, Pallas kernels, attend(): pl.pallas_call(functools.partial(attend_kernel, groups, heads, first_head...  80.6 us
    ppermute x24, waiting for transfers between devices, turn(): lax.ppermute(array, 'head', [(i, (i + shift) % groups) for i in range(gro...  70.1 us
    ppermute x4, waiting for transfers between devices, on_device(): before = lax.ppermute(own, 'seq', onward)  39.3 us
    ppermute x4, starting transfers between devices, on_device(): before = lax.ppermute(own, 'seq', onward)  11 us
    pallas_call x4, Pallas kernels, pack(): pl.pallas_call(kernel, in_specs=[ANY] * (3 + len(after)), out_specs=[ANY]...  10.6 us
    unnamed x97, local copies, waits for them, and re-layouts  9.83 us
    pallas_call x4, Pallas kernels, assemble(): pl.pallas_call(kernel, in_specs=[ANY] * (groups + len(after)), out_specs=...  8.87 us
  transfers between devices with their start and end apart: 32, of which 9 were waited for; matrix products, arithmetic and copies ran while one was open for 1% of the time, Pallas kernels for 28%

profile of v1, /device:TPU:6, one launch (start us, length us, event | category | flops | bytes accessed | tf_op | source)
XLA Modules:
  0.0 327.8 jit_solution(17452828110177607470)
XLA Ops:
  0.0 2.8 pack.5
  4.4 2.6 collective-permute-start.4
  8.4 2.9 pack.4
  11.2 11.6 %collective-permute-done.3.refs_1_.refs_2_ = bf16[288,1152]{1,0:T(8,128)(2,1)S(1)} collective-permute-done((bf16[288,1152]{1,0:T(8,128)(2,1)}, bf16[288,1152]{1,0:T(8,128)(2,1)S(1)}, u32[]{:S(2)}, u32[]{:S(2)}) %collective-permute-start.3) | collective-permute-done | bytes 663584 | tf_op jit(solution)/shard_map/ppermute | solution.py:297
  22.8 27.4 %collective-permute-done.4.refs_2_.refs_3_ = bf16[288,1152]{1,0:T(8,128)(2,1)S(1)} collective-permute-done((bf16[288,1152]{1,0:T(8,128)(2,1)}, bf16[288,1152]{1,0:T(8,128)(2,1)S(1)}, u32[]{:S(2)}, u32[]{:S(2)}) %collective-permute-start.4) | collective-permute-done | bytes 663584 | tf_op jit(solution)/shard_map/ppermute | solution.py:297
  51.3 2.3 assemble.4.refs_3_.refs_6_
  55.6 3.6 %collective-permute-start.6 = (bf16[1152,768]{1,0:T(8,128)(2,1)}, bf16[1152,768]{1,0:T(8,128)(2,1)}, u32[]{:S(2)}, u32[]{:S(2)}) collective-permute-start(bf16[1152,768]{1,0:T(8,128)(2,1)} %assemble.4.refs_3_.refs_6_), channel_id=1, source_target_pairs={{0,4},{4,8},{8,12},{12,16},{16,20},{20,24},{24,28},{1,5},{5,9},{9,... | collective-permute-start | bytes 5308424 | tf_op jit(solution)/shard_map/ppermute | solution.py:317
  59.1 14.5 %collective-permute-start = (bf16[288,1152]{1,0:T(8,128)(2,1)}, bf16[288,1152]{1,0:T(8,128)(2,1)S(1)}, u32[]{:S(2)}, u32[]{:S(2)}) collective-permute-start(bf16[288,1152]{1,0:T(8,128)(2,1)} %get-tuple-element.38), channel_id=1, source_target_pairs={{0,1},{1,2},{2,3},{3,0},{4,5},{5,6},{6,7},{7,4},{8,9},{9,10},{10,1... | collective-permute-start | bytes 1990664 | tf_op jit(solution)/shard_map/ppermute | solution.py:297
  77.8 2.5 pack.6
  80.3 16.4 %collective-permute-done.6.refs_5_ = bf16[1152,768]{1,0:T(8,128)(2,1)} collective-permute-done((bf16[1152,768]{1,0:T(8,128)(2,1)}, bf16[1152,768]{1,0:T(8,128)(2,1)}, u32[]{:S(2)}, u32[]{:S(2)}) %collective-permute-start.6) | collective-permute-done | bytes 1769504 | tf_op jit(solution)/shard_map/ppermute | solution.py:317
  96.7 22.6 %attend.4 = (bf16[288,384]{1,0:T(8,128)(2,1)}, bf16[288,384]{1,0:T(8,128)(2,1)}, bf16[288,384]{1,0:T(8,128)(2,1)}, bf16[288,384]{1,0:T(8,128)(2,1)}) custom-call(s32[27]{0:T(128)} %reshape.42.refs_0_, bf16[288,1152]{1,0:T(8,128)(2,1)} %get-tuple-element.41.refs_0_.refs_1_, bf16[288,1152]{1,0:T(8,128)(2,1)} %copy-done.3, bf16[288,1152]{1,0:T(8,128)(2,1)} %copy-done.4, ...), custom_call_target="tpu_custom_call" | custom-call | flops 24461180928 | bytes 7077888 | tf_op jit(solution)/shard_map/attend/pallas_call | solution.py:253
  120.6 2.4 assemble.5.refs_3_.refs_6_
  125.0 2.5 collective-permute-start.14
  127.5 14.6 %collective-permute-start.11 = (bf16[288,768]{1,0:T(8,128)(2,1)S(1)}, bf16[288,768]{1,0:T(8,128)(2,1)S(1)}, u32[]{:S(2)}, u32[]{:S(2)}) collective-permute-start(bf16[288,768]{1,0:T(8,128)(2,1)S(1)} %copy-done.36), channel_id=1, source_target_pairs={{0,1},{1,2},{2,3},{3,0},{4,5},{5,6},{6,7},{7,4},{8,9},{9,10},{10,1... | collective-permute-start | bytes 1327112 | tf_op jit(solution)/shard_map/ppermute | solution.py:297
  144.5 2.5 pack.7
  147.1 17.8 %collective-permute-done.14.refs_5_ = bf16[1152,768]{1,0:T(8,128)(2,1)S(1)} collective-permute-done((bf16[1152,768]{1,0:T(8,128)(2,1)}, bf16[1152,768]{1,0:T(8,128)(2,1)S(1)}, u32[]{:S(2)}, u32[]{:S(2)}) %collective-permute-start.14) | collective-permute-done | bytes 1769504 | tf_op jit(solution)/shard_map/ppermute | solution.py:317
  166.0 22.5 %attend.5 = (bf16[288,384]{1,0:T(8,128)(2,1)}, bf16[288,384]{1,0:T(8,128)(2,1)}, bf16[288,384]{1,0:T(8,128)(2,1)}, bf16[288,384]{1,0:T(8,128)(2,1)}) custom-call(s32[27]{0:T(128)} %reshape.42.refs_0_, bf16[288,1152]{1,0:T(8,128)(2,1)} %get-tuple-element.37.refs_4_.refs_0_.refs_1_, bf16[288,1152]{1,0:T(8,128)(2,1)} %copy-done, bf16[288,1152]{1,0:T(8,128)(2,1)} %copy-done.1, ...), custom_call_target="tpu_custom_call" | custom-call | flops 24461180928 | bytes 7077888 | tf_op jit(solution)/shard_map/attend/pallas_call | solution.py:253
  193.7 2.5 collective-permute-start.16
  196.2 14.6 %collective-permute-start.8 = (bf16[288,768]{1,0:T(8,128)(2,1)S(1)}, bf16[288,768]{1,0:T(8,128)(2,1)S(1)}, u32[]{:S(2)}, u32[]{:S(2)}) collective-permute-start(bf16[288,768]{1,0:T(8,128)(2,1)S(1)} %copy-done.38), channel_id=1, source_target_pairs={{0,1},{1,2},{2,3},{3,0},{4,5},{5,6},{6,7},{7,4},{8,9},{9,10},{10,1... | collective-permute-start | bytes 1327112 | tf_op jit(solution)/shard_map/ppermute | solution.py:297
  213.2 5.1 %collective-permute-done.16.refs_5_ = bf16[1152,512]{1,0:T(8,128)(2,1)S(1)} collective-permute-done((bf16[1152,512]{1,0:T(8,128)(2,1)}, bf16[1152,512]{1,0:T(8,128)(2,1)S(1)}, u32[]{:S(2)}, u32[]{:S(2)}) %collective-permute-start.16) | collective-permute-done | bytes 1179680 | tf_op jit(solution)/shard_map/ppermute | solution.py:317
  219.3 17.8 %attend.6 = (bf16[288,256]{1,0:T(8,128)(2,1)}, bf16[288,256]{1,0:T(8,128)(2,1)}, bf16[288,256]{1,0:T(8,128)(2,1)}, bf16[288,256]{1,0:T(8,128)(2,1)}) custom-call(s32[27]{0:T(128)} %reshape.42.refs_0_, bf16[288,768]{1,0:T(8,128)(2,1)} %get-tuple-element.45.refs_9_.refs_4_.refs_0_.refs_1_, bf16[288,768]{1,0:T(8,128)(2,1)} %copy-done.9, ...), custom_call_target="tpu_custom_call" | custom-call | flops 16307453952 | bytes 4718592 | tf_op jit(solution)/shard_map/attend/pallas_call | solution.py:253
  237.2 3.0 collective-permute-done.9.refs_2_.refs_3_
  245.1 2.5 collective-permute-start.18
  247.6 12.4 %collective-permute-start.23 = (bf16[288,384]{1,0:T(8,128)(2,1)S(1)}, bf16[288,384]{1,0:T(8,128)(2,1)S(1)}, u32[]{:S(2)}, u32[]{:S(2)}) collective-permute-start(bf16[288,384]{1,0:T(8,128)(2,1)S(1)} %copy-done.43), channel_id=1, source_target_pairs={{0,3},{1,0},{2,1},{3,2},{4,7},{5,4},{6,5},{7,6},{8,11},{9,8},{10,9... | collective-permute-start | bytes 663560 | tf_op jit(solution)/shard_map/ppermute | solution.py:297
  261.0 4.9 %collective-permute-done.23.refs_1_ = bf16[288,384]{1,0:T(8,128)(2,1)S(1)} collective-permute-done((bf16[288,384]{1,0:T(8,128)(2,1)S(1)}, bf16[288,384]{1,0:T(8,128)(2,1)S(1)}, u32[]{:S(2)}, u32[]{:S(2)}) %collective-permute-start.23) | collective-permute-done | bytes 221216 | tf_op jit(solution)/shard_map/ppermute | solution.py:297
  265.9 4.3 %collective-permute-start.26 = (bf16[288,384]{1,0:T(8,128)(2,1)S(1)}, bf16[288,384]{1,0:T(8,128)(2,1)S(1)}, u32[]{:S(2)}, u32[]{:S(2)}) collective-permute-start(bf16[288,384]{1,0:T(8,128)(2,1)S(1)} %copy-done.44), channel_id=1, source_target_pairs={{0,3},{1,0},{2,1},{3,2},{4,7},{5,4},{6,5},{7,6},{8,11},{9,8},{10,9... | collective-permute-start | bytes 663560 | tf_op jit(solution)/shard_map/ppermute | solution.py:297
  270.2 13.7 %collective-permute-done.24.refs_2_ = bf16[288,384]{1,0:T(8,128)(2,1)S(1)} collective-permute-done((bf16[288,384]{1,0:T(8,128)(2,1)S(1)}, bf16[288,384]{1,0:T(8,128)(2,1)S(1)}, u32[]{:S(2)}, u32[]{:S(2)}) %collective-permute-start.24) | collective-permute-done | bytes 221216 | tf_op jit(solution)/shard_map/ppermute | solution.py:297
  284.1 3.8 %collective-permute-start.29 = (bf16[288,256]{1,0:T(8,128)(2,1)S(1)}, bf16[288,256]{1,0:T(8,128)(2,1)S(1)}, u32[]{:S(2)}, u32[]{:S(2)}) collective-permute-start(bf16[288,256]{1,0:T(8,128)(2,1)S(1)} %copy-done.47), channel_id=1, source_target_pairs={{0,3},{1,0},{2,1},{3,2},{4,7},{5,4},{6,5},{7,6},{8,11},{9,8},{10,9... | collective-permute-start | bytes 442376 | tf_op jit(solution)/shard_map/ppermute | solution.py:297
  287.9 17.8 %attend.7 = (bf16[288,256]{1,0:T(8,128)(2,1)}, bf16[288,256]{1,0:T(8,128)(2,1)}, bf16[288,256]{1,0:T(8,128)(2,1)}, bf16[288,256]{1,0:T(8,128)(2,1)}) custom-call(s32[27]{0:T(128)} %reshape.42.refs_0_, bf16[288,768]{1,0:T(8,128)(2,1)} %get-tuple-element.47.refs_9_.refs_4_.refs_0_.refs_1_, bf16[288,768]{1,0:T(8,128)(2,1)} %copy-done.6, ...), custom_call_target="tpu_custom_call" | custom-call | flops 16307453952 | bytes 4718592 | tf_op jit(solution)/shard_map/attend/pallas_call | solution.py:253
  307.4 3.4 %collective-permute-start.20 = (bf16[288,256]{1,0:T(8,128)(2,1)}, bf16[288,256]{1,0:T(8,128)(2,1)S(1)}, u32[]{:S(2)}, u32[]{:S(2)}) collective-permute-start(bf16[288,256]{1,0:T(8,128)(2,1)} %get-tuple-element.57), channel_id=1, source_target_pairs={{0,3},{1,0},{2,1},{3,2},{4,7},{5,4},{6,5},{7,6},{8,11},{9,8},{10,9... | collective-permute-start | bytes 442376 | tf_op jit(solution)/shard_map/ppermute | solution.py:297
  311.4 9.6 %collective-permute-done.30.refs_10_ = bf16[288,256]{1,0:T(8,128)(2,1)S(1)} collective-permute-done((bf16[288,256]{1,0:T(8,128)(2,1)S(1)}, bf16[288,256]{1,0:T(8,128)(2,1)S(1)}, u32[]{:S(2)}, u32[]{:S(2)}) %collective-permute-start.30) | collective-permute-done | bytes 147488 | tf_op jit(solution)/shard_map/ppermute | solution.py:297
  322.3 2.6 place.2.refs_4_
  (147 shorter events, 38.0 us)
Async XLA Ops:
  2.8 20.0 %collective-permute-start.3 = (bf16[288,1152]{1,0:T(8,128)(2,1)}, bf16[288,1152]{1,0:T(8,128)(2,1)S(1)}, u32[]{:S(2)}, u32[]{:S(2)}) collective-permute-start(bf16[288,1152]{1,0:T(8,128)(2,1)} %get-tuple-element.42), channel_id=1, source_target_pairs={{0,1},{1,2},{2,3},{3,0},{4,5},{5,6},{6,7},{7,4},{8,9},{9,10},{10,1... | collective-permute-start | bytes 1990664 | tf_op jit(solution)/shard_map/ppermute | solution.py:297
  4.4 45.7 %collective-permute-start.4 = (bf16[288,1152]{1,0:T(8,128)(2,1)}, bf16[288,1152]{1,0:T(8,128)(2,1)S(1)}, u32[]{:S(2)}, u32[]{:S(2)}) collective-permute-start(bf16[288,1152]{1,0:T(8,128)(2,1)} %get-tuple-element.43), channel_id=1, source_target_pairs={{0,2},{1,3},{2,0},{3,1},{4,6},{5,7},{6,4},{7,5},{8,10},{9,11},{10,... | collective-permute-start | bytes 1990664 | tf_op jit(solution)/shard_map/ppermute | solution.py:297
  7.0 43.1 %collective-permute-start.5 = (bf16[288,1152]{1,0:T(8,128)(2,1)}, bf16[288,1152]{1,0:T(8,128)(2,1)S(1)}, u32[]{:S(2)}, u32[]{:S(2)}) collective-permute-start(bf16[288,1152]{1,0:T(8,128)(2,1)} %get-tuple-element.44), channel_id=1, source_target_pairs={{0,3},{1,0},{2,1},{3,2},{4,7},{5,4},{6,5},{7,6},{8,11},{9,8},{10,9... | collective-permute-start | bytes 1990664 | tf_op jit(solution)/shard_map/ppermute | solution.py:297
  53.6 26.7 %collective-permute-start.7 = (bf16[1152,768]{1,0:T(8,128)(2,1)}, bf16[1152,768]{1,0:T(8,128)(2,1)}, u32[]{:S(2)}, u32[]{:S(2)}) collective-permute-start(bf16[1152,768]{1,0:T(8,128)(2,1)} %assemble.4.refs_3_.refs_6_), channel_id=1, source_target_pairs={{4,0},{8,4},{12,8},{16,12},{20,16},{24,20},{28,24},{5,1},{9,5},{13... | collective-permute-start | bytes 5308424 | tf_op jit(solution)/shard_map/ppermute | solution.py:318
  55.6 41.2 %collective-permute-start.6 = (bf16[1152,768]{1,0:T(8,128)(2,1)}, bf16[1152,768]{1,0:T(8,128)(2,1)}, u32[]{:S(2)}, u32[]{:S(2)}) collective-permute-start(bf16[1152,768]{1,0:T(8,128)(2,1)} %assemble.4.refs_3_.refs_6_), channel_id=1, source_target_pairs={{0,4},{4,8},{8,12},{12,16},{16,20},{20,24},{24,28},{1,5},{5,9},{9,... | collective-permute-start | bytes 5308424 | tf_op jit(solution)/shard_map/ppermute | solution.py:317
  59.1 60.2 %collective-permute-start = (bf16[288,1152]{1,0:T(8,128)(2,1)}, bf16[288,1152]{1,0:T(8,128)(2,1)S(1)}, u32[]{:S(2)}, u32[]{:S(2)}) collective-permute-start(bf16[288,1152]{1,0:T(8,128)(2,1)} %get-tuple-element.38), channel_id=1, source_target_pairs={{0,1},{1,2},{2,3},{3,0},{4,5},{5,6},{6,7},{7,4},{8,9},{9,10},{10,1... | collective-permute-start | bytes 1990664 | tf_op jit(solution)/shard_map/ppermute | solution.py:297
  73.6 45.7 %collective-permute-start.1 = (bf16[288,1152]{1,0:T(8,128)(2,1)}, bf16[288,1152]{1,0:T(8,128)(2,1)S(1)}, u32[]{:S(2)}, u32[]{:S(2)}) collective-permute-start(bf16[288,1152]{1,0:T(8,128)(2,1)} %get-tuple-element.39), channel_id=1, source_target_pairs={{0,2},{1,3},{2,0},{3,1},{4,6},{5,7},{6,4},{7,5},{8,10},{9,11},{10,... | collective-permute-start | bytes 1990664 | tf_op jit(solution)/shard_map/ppermute | solution.py:297
  75.5 43.9 %collective-permute-start.2 = (bf16[288,1152]{1,0:T(8,128)(2,1)}, bf16[288,1152]{1,0:T(8,128)(2,1)S(1)}, u32[]{:S(2)}, u32[]{:S(2)}) collective-permute-start(bf16[288,1152]{1,0:T(8,128)(2,1)} %get-tuple-element.40), channel_id=1, source_target_pairs={{0,3},{1,0},{2,1},{3,2},{4,7},{5,4},{6,5},{7,6},{8,11},{9,8},{10,9... | collective-permute-start | bytes 1990664 | tf_op jit(solution)/shard_map/ppermute | solution.py:297
  123.0 24.0 %collective-permute-start.15 = (bf16[1152,768]{1,0:T(8,128)(2,1)}, bf16[1152,768]{1,0:T(8,128)(2,1)S(1)}, u32[]{:S(2)}, u32[]{:S(2)}) collective-permute-start(bf16[1152,768]{1,0:T(8,128)(2,1)} %assemble.5.refs_3_.refs_6_), channel_id=1, source_target_pairs={{4,0},{8,4},{12,8},{16,12},{20,16},{24,20},{28,24},{5,1},{9,5},{13... | collective-permute-start | bytes 5308424 | tf_op jit(solution)/shard_map/ppermute | solution.py:318
  125.0 39.8 %collective-permute-start.14 = (bf16[1152,768]{1,0:T(8,128)(2,1)}, bf16[1152,768]{1,0:T(8,128)(2,1)S(1)}, u32[]{:S(2)}, u32[]{:S(2)}) collective-permute-start(bf16[1152,768]{1,0:T(8,128)(2,1)} %assemble.5.refs_3_.refs_6_), channel_id=1, source_target_pairs={{0,4},{4,8},{8,12},{12,16},{16,20},{20,24},{24,28},{1,5},{5,9},{9,... | collective-permute-start | bytes 5308424 | tf_op jit(solution)/shard_map/ppermute | solution.py:317
  127.5 61.0 %collective-permute-start.11 = (bf16[288,768]{1,0:T(8,128)(2,1)S(1)}, bf16[288,768]{1,0:T(8,128)(2,1)S(1)}, u32[]{:S(2)}, u32[]{:S(2)}) collective-permute-start(bf16[288,768]{1,0:T(8,128)(2,1)S(1)} %copy-done.36), channel_id=1, source_target_pairs={{0,1},{1,2},{2,3},{3,0},{4,5},{5,6},{6,7},{7,4},{8,9},{9,10},{10,1... | collective-permute-start | bytes 1327112 | tf_op jit(solution)/shard_map/ppermute | solution.py:297
  142.1 46.5 %collective-permute-start.12 = (bf16[288,768]{1,0:T(8,128)(2,1)S(1)}, bf16[288,768]{1,0:T(8,128)(2,1)S(1)}, u32[]{:S(2)}, u32[]{:S(2)}) collective-permute-start(bf16[288,768]{1,0:T(8,128)(2,1)S(1)} %copy-done.34), channel_id=1, source_target_pairs={{0,2},{1,3},{2,0},{3,1},{4,6},{5,7},{6,4},{7,5},{8,10},{9,11},{10,... | collective-permute-start | bytes 1327112 | tf_op jit(solution)/shard_map/ppermute | solution.py:297
  142.9 45.7 %collective-permute-start.13 = (bf16[288,768]{1,0:T(8,128)(2,1)S(1)}, bf16[288,768]{1,0:T(8,128)(2,1)S(1)}, u32[]{:S(2)}, u32[]{:S(2)}) collective-permute-start(bf16[288,768]{1,0:T(8,128)(2,1)S(1)} %copy-done.33), channel_id=1, source_target_pairs={{0,3},{1,0},{2,1},{3,2},{4,7},{5,4},{6,5},{7,6},{8,11},{9,8},{10,9... | collective-permute-start | bytes 1327112 | tf_op jit(solution)/shard_map/ppermute | solution.py:297
  191.7 21.5 %collective-permute-start.17 = (bf16[1152,512]{1,0:T(8,128)(2,1)}, bf16[1152,512]{1,0:T(8,128)(2,1)S(1)}, u32[]{:S(2)}, u32[]{:S(2)}) collective-permute-start(bf16[1152,512]{1,0:T(8,128)(2,1)} %assemble.6.refs_6_), channel_id=1, source_target_pairs={{4,0},{8,4},{12,8},{16,12},{20,16},{24,20},{28,24},{5,1},{9,5},{13... | collective-permute-start | bytes 3538952 | tf_op jit(solution)/shard_map/ppermute | solution.py:318
  193.7 24.6 %collective-permute-start.16 = (bf16[1152,512]{1,0:T(8,128)(2,1)}, bf16[1152,512]{1,0:T(8,128)(2,1)S(1)}, u32[]{:S(2)}, u32[]{:S(2)}) collective-permute-start(bf16[1152,512]{1,0:T(8,128)(2,1)} %assemble.6.refs_6_), channel_id=1, source_target_pairs={{0,4},{4,8},{8,12},{12,16},{16,20},{20,24},{24,28},{1,5},{5,9},{9,... | collective-permute-start | bytes 3538952 | tf_op jit(solution)/shard_map/ppermute | solution.py:317
  196.2 41.0 %collective-permute-start.8 = (bf16[288,768]{1,0:T(8,128)(2,1)S(1)}, bf16[288,768]{1,0:T(8,128)(2,1)S(1)}, u32[]{:S(2)}, u32[]{:S(2)}) collective-permute-start(bf16[288,768]{1,0:T(8,128)(2,1)S(1)} %copy-done.38), channel_id=1, source_target_pairs={{0,1},{1,2},{2,3},{3,0},{4,5},{5,6},{6,7},{7,4},{8,9},{9,10},{10,1... | collective-permute-start | bytes 1327112 | tf_op jit(solution)/shard_map/ppermute | solution.py:297
  210.7 29.4 %collective-permute-start.9 = (bf16[288,768]{1,0:T(8,128)(2,1)S(1)}, bf16[288,768]{1,0:T(8,128)(2,1)S(1)}, u32[]{:S(2)}, u32[]{:S(2)}) collective-permute-start(bf16[288,768]{1,0:T(8,128)(2,1)S(1)} %copy-done.37), channel_id=1, source_target_pairs={{0,2},{1,3},{2,0},{3,1},{4,6},{5,7},{6,4},{7,5},{8,10},{9,11},{10,... | collective-permute-start | bytes 1327112 | tf_op jit(solution)/shard_map/ppermute | solution.py:297
  211.9 28.2 %collective-permute-start.10 = (bf16[288,768]{1,0:T(8,128)(2,1)S(1)}, bf16[288,768]{1,0:T(8,128)(2,1)S(1)}, u32[]{:S(2)}, u32[]{:S(2)}) collective-permute-start(bf16[288,768]{1,0:T(8,128)(2,1)S(1)} %copy-done.35), channel_id=1, source_target_pairs={{0,3},{1,0},{2,1},{3,2},{4,7},{5,4},{6,5},{7,6},{8,11},{9,8},{10,9... | collective-permute-start | bytes 1327112 | tf_op jit(solution)/shard_map/ppermute | solution.py:297
  243.1 40.8 %collective-permute-start.19 = (bf16[1152,512]{1,0:T(8,128)(2,1)}, bf16[1152,512]{1,0:T(8,128)(2,1)S(1)}, u32[]{:S(2)}, u32[]{:S(2)}) collective-permute-start(bf16[1152,512]{1,0:T(8,128)(2,1)} %assemble.7.refs_6_), channel_id=1, source_target_pairs={{4,0},{8,4},{12,8},{16,12},{20,16},{24,20},{28,24},{5,1},{9,5},{13... | collective-permute-start | bytes 3538952 | tf_op jit(solution)/shard_map/ppermute | solution.py:318
  245.1 38.9 %collective-permute-start.18 = (bf16[1152,512]{1,0:T(8,128)(2,1)}, bf16[1152,512]{1,0:T(8,128)(2,1)S(1)}, u32[]{:S(2)}, u32[]{:S(2)}) collective-permute-start(bf16[1152,512]{1,0:T(8,128)(2,1)} %assemble.7.refs_6_), channel_id=1, source_target_pairs={{0,4},{4,8},{8,12},{12,16},{16,20},{20,24},{24,28},{1,5},{5,9},{9,... | collective-permute-start | bytes 3538952 | tf_op jit(solution)/shard_map/ppermute | solution.py:317
  247.6 18.3 %collective-permute-start.23 = (bf16[288,384]{1,0:T(8,128)(2,1)S(1)}, bf16[288,384]{1,0:T(8,128)(2,1)S(1)}, u32[]{:S(2)}, u32[]{:S(2)}) collective-permute-start(bf16[288,384]{1,0:T(8,128)(2,1)S(1)} %copy-done.43), channel_id=1, source_target_pairs={{0,3},{1,0},{2,1},{3,2},{4,7},{5,4},{6,5},{7,6},{8,11},{9,8},{10,9... | collective-permute-start | bytes 663560 | tf_op jit(solution)/shard_map/ppermute | solution.py:297
  260.0 23.9 %collective-permute-start.24 = (bf16[288,384]{1,0:T(8,128)(2,1)S(1)}, bf16[288,384]{1,0:T(8,128)(2,1)S(1)}, u32[]{:S(2)}, u32[]{:S(2)}) collective-permute-start(bf16[288,384]{1,0:T(8,128)(2,1)S(1)} %copy-done.41), channel_id=1, source_target_pairs={{0,2},{1,3},{2,0},{3,1},{4,6},{5,7},{6,4},{7,5},{8,10},{9,11},{10,... | collective-permute-start | bytes 663560 | tf_op jit(solution)/shard_map/ppermute | solution.py:297
  261.0 44.7 %collective-permute-start.25 = (bf16[288,384]{1,0:T(8,128)(2,1)S(1)}, bf16[288,384]{1,0:T(8,128)(2,1)S(1)}, u32[]{:S(2)}, u32[]{:S(2)}) collective-permute-start(bf16[288,384]{1,0:T(8,128)(2,1)S(1)} %copy-done.39), channel_id=1, source_target_pairs={{0,1},{1,2},{2,3},{3,0},{4,5},{5,6},{6,7},{7,4},{8,9},{9,10},{10,1... | collective-permute-start | bytes 663560 | tf_op jit(solution)/shard_map/ppermute | solution.py:297
  265.9 41.0 %collective-permute-start.26 = (bf16[288,384]{1,0:T(8,128)(2,1)S(1)}, bf16[288,384]{1,0:T(8,128)(2,1)S(1)}, u32[]{:S(2)}, u32[]{:S(2)}) collective-permute-start(bf16[288,384]{1,0:T(8,128)(2,1)S(1)} %copy-done.44), channel_id=1, source_target_pairs={{0,3},{1,0},{2,1},{3,2},{4,7},{5,4},{6,5},{7,6},{8,11},{9,8},{10,9... | collective-permute-start | bytes 663560 | tf_op jit(solution)/shard_map/ppermute | solution.py:297
  283.9 23.4 %collective-permute-start.27 = (bf16[288,384]{1,0:T(8,128)(2,1)S(1)}, bf16[288,384]{1,0:T(8,128)(2,1)S(1)}, u32[]{:S(2)}, u32[]{:S(2)}) collective-permute-start(bf16[288,384]{1,0:T(8,128)(2,1)S(1)} %copy-done.42), channel_id=1, source_target_pairs={{0,2},{1,3},{2,0},{3,1},{4,6},{5,7},{6,4},{7,5},{8,10},{9,11},{10,... | collective-permute-start | bytes 663560 | tf_op jit(solution)/shard_map/ppermute | solution.py:297
  284.0 26.8 %collective-permute-start.28 = (bf16[288,384]{1,0:T(8,128)(2,1)S(1)}, bf16[288,384]{1,0:T(8,128)(2,1)S(1)}, u32[]{:S(2)}, u32[]{:S(2)}) collective-permute-start(bf16[288,384]{1,0:T(8,128)(2,1)S(1)} %copy-done.40), channel_id=1, source_target_pairs={{0,1},{1,2},{2,3},{3,0},{4,5},{5,6},{6,7},{7,4},{8,9},{9,10},{10,1... | collective-permute-start | bytes 663560 | tf_op jit(solution)/shard_map/ppermute | solution.py:297
  284.1 26.7 %collective-permute-start.29 = (bf16[288,256]{1,0:T(8,128)(2,1)S(1)}, bf16[288,256]{1,0:T(8,128)(2,1)S(1)}, u32[]{:S(2)}, u32[]{:S(2)}) collective-permute-start(bf16[288,256]{1,0:T(8,128)(2,1)S(1)} %copy-done.47), channel_id=1, source_target_pairs={{0,3},{1,0},{2,1},{3,2},{4,7},{5,4},{6,5},{7,6},{8,11},{9,8},{10,9... | collective-permute-start | bytes 442376 | tf_op jit(solution)/shard_map/ppermute | solution.py:297
  305.7 15.3 %collective-permute-start.30 = (bf16[288,256]{1,0:T(8,128)(2,1)S(1)}, bf16[288,256]{1,0:T(8,128)(2,1)S(1)}, u32[]{:S(2)}, u32[]{:S(2)}) collective-permute-start(bf16[288,256]{1,0:T(8,128)(2,1)S(1)} %copy-done.46), channel_id=1, source_target_pairs={{0,2},{1,3},{2,0},{3,1},{4,6},{5,7},{6,4},{7,5},{8,10},{9,11},{10,... | collective-permute-start | bytes 442376 | tf_op jit(solution)/shard_map/ppermute | solution.py:297
  306.9 14.1 %collective-permute-start.31 = (bf16[288,256]{1,0:T(8,128)(2,1)S(1)}, bf16[288,256]{1,0:T(8,128)(2,1)S(1)}, u32[]{:S(2)}, u32[]{:S(2)}) collective-permute-start(bf16[288,256]{1,0:T(8,128)(2,1)S(1)} %copy-done.45), channel_id=1, source_target_pairs={{0,1},{1,2},{2,3},{3,0},{4,5},{5,6},{6,7},{7,4},{8,9},{9,10},{10,1... | collective-permute-start | bytes 442376 | tf_op jit(solution)/shard_map/ppermute | solution.py:297
  307.4 17.6 %collective-permute-start.20 = (bf16[288,256]{1,0:T(8,128)(2,1)}, bf16[288,256]{1,0:T(8,128)(2,1)S(1)}, u32[]{:S(2)}, u32[]{:S(2)}) collective-permute-start(bf16[288,256]{1,0:T(8,128)(2,1)} %get-tuple-element.57), channel_id=1, source_target_pairs={{0,3},{1,0},{2,1},{3,2},{4,7},{5,4},{6,5},{7,6},{8,11},{9,8},{10,9... | collective-permute-start | bytes 442376 | tf_op jit(solution)/shard_map/ppermute | solution.py:297
  310.8 14.2 %collective-permute-start.21 = (bf16[288,256]{1,0:T(8,128)(2,1)}, bf16[288,256]{1,0:T(8,128)(2,1)S(1)}, u32[]{:S(2)}, u32[]{:S(2)}) collective-permute-start(bf16[288,256]{1,0:T(8,128)(2,1)} %get-tuple-element.58), channel_id=1, source_target_pairs={{0,2},{1,3},{2,0},{3,1},{4,6},{5,7},{6,4},{7,5},{8,10},{9,11},{10,... | collective-permute-start | bytes 442376 | tf_op jit(solution)/shard_map/ppermute | solution.py:297
  310.8 14.2 %collective-permute-start.22 = (bf16[288,256]{1,0:T(8,128)(2,1)}, bf16[288,256]{1,0:T(8,128)(2,1)S(1)}, u32[]{:S(2)}, u32[]{:S(2)}) collective-permute-start(bf16[288,256]{1,0:T(8,128)(2,1)} %get-tuple-element.59), channel_id=1, source_target_pairs={{0,1},{1,2},{2,3},{3,0},{4,5},{5,6},{6,7},{7,4},{8,9},{9,10},{10,1... | collective-permute-start | bytes 442376 | tf_op jit(solution)/shard_map/ppermute | solution.py:297
  (48 other events, 648.3 us)

commit v2 on v1

--- a/solution.py
+++ b/solution.py
@@ -9,7 +9,7 @@
 from jax.sharding import PartitionSpec as P
 
 LANES = 128
-CHUNKS = 4
+CHUNK_HEADS = 3
 ANY = pl.BlockSpec(memory_space=pl.ANY)
 VMEM_LIMIT = 56 * 2**20
 
@@ -50,24 +50,20 @@
     rows = arrays[0].shape[0]
 
     def kernel(*refs):
-        sources, outs = refs[:3], refs[3 + len(after) : 3 + len(after) + groups]
-        stages, sems = refs[3 + len(after) + groups : -1], refs[-1]
-        me = lax.axis_index("head")
+        sources, out = refs[:3], refs[3 + len(after)]
+        stages, sems = refs[4 + len(after) : -1], refs[-1]
         pairs = []
-        for shift in range(groups):
-            group = lax.rem(me + shift, groups)
-            column = pl.multiple_of(group * group_width + start, LANES)
+        for group in range(groups):
+            columns = pl.ds(group * group_width + start, width)
             for i, source in enumerate(sources):
-                pairs.append(
-                    (source.at[:, pl.ds(column, width)], outs[shift].at[:, pl.ds(i * width, width)])
-                )
+                pairs.append((source.at[:, columns], out.at[group, :, pl.ds(i * width, width)]))
         staged(pairs, stages, sems)
 
     return pl.pallas_call(
         kernel,
         in_specs=[ANY] * (3 + len(after)),
-        out_specs=[ANY] * groups,
-        out_shape=[jax.ShapeDtypeStruct((rows, 3 * width), jnp.bfloat16)] * groups,
+        out_specs=ANY,
+        out_shape=jax.ShapeDtypeStruct((groups, rows, 3 * width), jnp.bfloat16),
         scratch_shapes=stage_shapes([(rows, width)] * (3 * groups)),
         cost_estimate=pl.CostEstimate(
             flops=0, bytes_accessed=12 * groups * rows * width, transcendentals=0
@@ -77,33 +73,19 @@
     )(*arrays, *after)
 
 
-def assemble(pieces, after, width):
-    groups = len(pieces)
-    rows = pieces[0].shape[0]
-
+def gate(array, after):
     def kernel(*refs):
-        parts, out = refs[:groups], refs[groups + len(after)]
-        stages, sems = refs[groups + len(after) + 1 : -1], refs[-1]
-        me = lax.axis_index("head")
-        pairs = []
-        for shift in range(groups):
-            owner = lax.rem(me + groups - shift, groups)
-            row = pl.multiple_of(owner * rows, 16)
-            pairs.append((parts[shift].at[:, pl.ds(0, 2 * width)], out.at[pl.ds(row, rows), :]))
-        staged(pairs, stages, sems)
+        del refs
 
     return pl.pallas_call(
         kernel,
-        in_specs=[ANY] * (groups + len(after)),
+        in_specs=[ANY] * (1 + len(after)),
         out_specs=ANY,
-        out_shape=jax.ShapeDtypeStruct((groups * rows, 2 * width), jnp.bfloat16),
-        scratch_shapes=stage_shapes([(rows, 2 * width)] * groups),
-        cost_estimate=pl.CostEstimate(
-            flops=0, bytes_accessed=8 * groups * rows * width, transcendentals=0
-        ),
+        out_shape=jax.ShapeDtypeStruct(array.shape, array.dtype),
+        input_output_aliases={0: 0},
         compiler_params=pltpu.CompilerParams(vmem_limit_bytes=VMEM_LIMIT),
-        name="assemble",
-    )(*pieces, *after)
+        name="gate",
+    )(array, *after)
 
 
 def place(chunks, group_width, total_width, target=None):
@@ -149,11 +131,10 @@
 
 
 def attend_kernel(groups, heads, first_head, tile_count, *refs):
-    plan_ref, pieces = refs[0], refs[1 : 1 + groups]
-    prev_ref, own_ref, next_ref, keep_ref = refs[1 + groups : 5 + groups]
-    outs = refs[-6 - groups : -6]
-    q_ref, out_ref, scores_ref, top_ref, total_ref, sum_ref = refs[-6:]
-    slab_rows, width = q_ref.shape
+    plan_ref, own_ref, prev_ref, next_ref, keep_ref = refs[:5]
+    outs = refs[-5 - groups : -5]
+    out_ref, scores_ref, top_ref, total_ref, sum_ref = refs[-5:]
+    slab_rows, width = out_ref.shape
     local_rows = slab_rows // groups
     head_size = width // heads
     tile_rows = slab_rows // tile_count
@@ -171,9 +152,6 @@
     def lanes(index):
         return pl.ds(index * head_size, head_size)
 
-    for shift in range(groups):
-        q_ref[owner_rows(shift), :] = pieces[shift][...]
-
     def one_tile(i, carry):
         top_ref[...] = jnp.full_like(top_ref, -jnp.inf)
         total_ref[...] = jnp.zeros_like(total_ref)
@@ -188,7 +166,7 @@
                 def _():
                     for h in range(heads):
                         found = lax.dot_general(
-                            q_ref[tile(i), lanes(h)],
+                            own_ref[tile(i), lanes(2 * heads + h)],
                             pair_ref[tile(place), lanes(h)],
                             (((1,), (1,)), ((), ())),
                             preferred_element_type=jnp.float32,
@@ -240,28 +218,25 @@
         outs[shift][...] = out_ref[owner_rows(shift), :]
 
 
-def attend(plan, pieces, prev, own, behind, keep_mask, after, first_head, heads, tile_count):
-    groups = len(pieces)
-    slab_rows = own.shape[0]
+def attend(plan, own, prev, behind, keep_mask, after, groups, first_head, heads, tile_count):
+    slab_rows, width = own.shape[0], own.shape[1] // 3
     local_rows = slab_rows // groups
-    width = own.shape[1] // 2
     tile_rows = slab_rows // tile_count
     head_size = width // heads
     pairs = heads * slab_rows * 3 * slab_rows
-    whole = pl.BlockSpec(own.shape, lambda s, plan: (0, 0))
+    wholes = [
+        pl.BlockSpec(array.shape, lambda s, plan: (0, 0))
+        for array in (own, prev, behind, keep_mask)
+    ]
     accumulator = pltpu.VMEM((heads, tile_rows, LANES), jnp.float32)
     return pl.pallas_call(
         functools.partial(attend_kernel, groups, heads, first_head, tile_count),
         grid_spec=pltpu.PrefetchScalarGridSpec(
             num_scalar_prefetch=1,
             grid=(1,),
-            in_specs=[pl.BlockSpec((local_rows, width), lambda s, plan: (0, 2))] * groups
-            + [whole] * 3
-            + [pl.BlockSpec(keep_mask.shape, lambda s, plan: (0, 0))]
-            + [ANY] * len(after),
+            in_specs=wholes + [ANY] * len(after),
             out_specs=[pl.BlockSpec((local_rows, width), lambda s, plan: (0, 0))] * groups,
             scratch_shapes=[
-                pltpu.VMEM((slab_rows, width), jnp.bfloat16),
                 pltpu.VMEM((slab_rows, width), jnp.bfloat16),
                 pltpu.VMEM((heads, 3 * tile_count, tile_rows, tile_rows), jnp.float32),
                 accumulator,
@@ -277,7 +252,7 @@
             transcendentals=pairs,
         ),
         name="attend",
-    )(plan, *pieces, prev, own, behind, keep_mask, *after)
+    )(plan, own, prev, behind, keep_mask, *after)
 
 
 def on_device(queries, key_vectors, value_vectors, reach_time, reach_width, keep_mask):
@@ -296,31 +271,37 @@
     def turn(array, shift):
         return lax.ppermute(array, "head", [(i, (i + shift) % groups) for i in range(groups)])
 
-    count = min(CHUNKS, group_heads)
-    sizes = [group_heads // count + (i < group_heads % count) for i in range(count)]
+    parts = -(-(group_heads - 1) // CHUNK_HEADS)
+    sizes = [(group_heads - 1 + i) // parts for i in reversed(range(parts))] + [1]
+    count = len(sizes)
     firsts = [sum(sizes[:i]) for i in range(count)]
     sources = (key_vectors, value_vectors, queries)
 
-    def send(i, after):
-        width = sizes[i] * head_size
-        blocks = pack(sources, after, groups, group_width, firsts[i] * head_size, width)
-        return [blocks[0]] + [turn(blocks[shift], shift) for shift in range(1, groups)]
-
-    pieces = [send(i, []) for i in range(min(2, count))]
-    done = []
+    def packed(i, after):
+        start, width = firsts[i] * head_size, sizes[i] * head_size
+        return pack(sources, after, groups, group_width, start, width)
+
+    def arrive(parts, after):
+        own = lax.all_to_all(parts, "head", split_axis=0, concat_axis=0, tiled=True)
+        own = gate(own, after) if after else own
+        own = own.reshape(-1, own.shape[2])
+        pairs = own[:, : own.shape[1] // 3 * 2]
+        return own, lax.ppermute(pairs, "seq", onward), lax.ppermute(pairs, "seq", backward)
+
+    sent = [packed(i, []) for i in range(min(2, count))]
+    there, done = [arrive(sent[0], [])], []
+    if count > 1:
+        sent[1] = gate(sent[1], there[0][:1])
     for i, heads in enumerate(sizes):
-        own = assemble(
-            pieces[i],
-            [part[0] for part in pieces[i + 1 :]] + [part[1][0] for part in done[-1:]],
-            heads * head_size,
-        )
-        before = lax.ppermute(own, "seq", onward)
-        behind = lax.ppermute(own, "seq", backward)
+        if i + 1 < count:
+            there.append(arrive(sent[i + 1], [part[1][0] for part in done[-1:]]))
         if i + 2 < count:
-            pieces.append(send(i + 2, [own]))
-        hold = [part[0] for part in pieces[i + 2 :]]
+            sent.append(gate(packed(i + 2, [there[i][0]]), there[i + 1][:1]))
+        hold = [part[0] for part in there[i + 1 :]] + sent[i + 2 :]
+        hold += [part[1][0] for part in done[-1:]]
+        hold += [block for part in done[-2:-1] for block in part[1][1:]]
         outs = attend(
-            plan, pieces[i], before, own, behind, keep_mask, hold, firsts[i], heads, tile_count
+            plan, *there[i], keep_mask, hold, groups, firsts[i], heads, tile_count
         )
         back = [outs[0]] + [turn(outs[shift], groups - shift) for shift in range(1, groups)]
         done.append((firsts[i] * head_size, back))

time: 333 us -> 322 us (0.967)
  the two profiles are of different devices: /device:TPU:6 before, /device:TPU:5 now
where the time goes in v2:
time: 322 us; the launch traced here: 325 us
  waiting for transfers between devices  129 us (40%)
  Pallas kernels  123 us (38%)
  starting transfers between devices  56.8 us (18%)
  local copies, waits for them, and re-layouts  15.6 us (5%)
    all_to_all x4, waiting for transfers between devices, arrive(): own = lax.all_to_all(parts, 'head', split_axis=0, concat_axis=0, tiled=True)  128 us
    pallas_call x4, Pallas kernels, attend(): pl.pallas_call(functools.partial(attend_kernel, groups, heads, first_head...  108 us
    all_to_all x4, starting transfers between devices, arrive(): own = lax.all_to_all(parts, 'head', split_axis=0, concat_axis=0, tiled=True)  16.7 us
    ppermute x4, starting transfers between devices, arrive(): lax.ppermute(pairs, 'seq', onward)  16.4 us
    ppermute x12, starting transfers between devices, turn(): lax.ppermute(array, 'head', [(i, (i + shift) % groups) for i in range(gro...  15.2 us
    pallas_call x4, Pallas kernels, pack(): pl.pallas_call(kernel, in_specs=[ANY] * (3 + len(after)), out_specs=ANY,...  10.5 us
    ppermute x4, starting transfers between devices, arrive(): lax.ppermute(pairs, 'seq', backward)  8.35 us
    unnamed x49, local copies, waits for them, and re-layouts  8.12 us
  transfers between devices with their start and end apart: 24, of which 4 were waited for; matrix products, arithmetic and copies ran while one was open for 3% of the time, Pallas kernels for 36%

profile of v2, /device:TPU:5, one launch (start us, length us, event | category | flops | bytes accessed | tf_op | source)
XLA Modules:
  0.0 324.6 jit_solution(15943496501743257649)
XLA Ops:
  0.0 2.8 pack.5
  2.8 4.6 %all-to-all-start = ((bf16[4,288,1152]{2,1,0:T(8,128)(2,1)}), bf16[4,288,1152]{2,1,0:T(8,128)(2,1)S(1)}, u32[]{:S(2)}, u32[]{:S(2)}) async-start(bf16[4,288,1152]{2,1,0:T(8,128)(2,1)} %pack.5), calls=%async_computation | async-start | bytes 5308416 | tf_op jit(solution)/shard_map/all_to_all | solution.py:285
  7.4 2.7 pack.4.refs_0_
  10.2 56.9 %all-to-all-done = bf16[4,288,1152]{2,1,0:T(8,128)(2,1)S(1)} async-done(((bf16[4,288,1152]{2,1,0:T(8,128)(2,1)}), bf16[4,288,1152]{2,1,0:T(8,128)(2,1)S(1)}, u32[]{:S(2)}, u32[]{:S(2)}) %all-to-all-start) | async-done | bytes 2654240 | tf_op jit(solution)/shard_map/all_to_all | solution.py:285
  68.6 4.8 %all-to-all-start.1 = ((bf16[4,288,1152]{2,1,0:T(8,128)(2,1)}), bf16[4,288,1152]{2,1,0:T(8,128)(2,1)}, u32[]{:S(2)}, u32[]{:S(2)}) async-start(bf16[4,288,1152]{2,1,0:T(8,128)(2,1)} %gate.5), calls=%async_computation.1 | async-start | bytes 5308416 | tf_op jit(solution)/shard_map/all_to_all | solution.py:285
  74.8 4.4 %collective-permute-start = (bf16[1152,768]{1,0:T(8,128)(2,1)}, bf16[1152,768]{1,0:T(8,128)(2,1)}, u32[]{:S(2)}, u32[]{:S(2)}) collective-permute-start(bf16[1152,768]{1,0:T(8,128)(2,1)} %slice.16), channel_id=1, source_target_pairs={{0,4},{4,8},{8,12},{12,16},{16,20},{20,24},{24,28},{1,5},{5,9},{9,... | collective-permute-start | bytes 5308424 | tf_op jit(solution)/shard_map/ppermute | solution.py:289
  79.3 1.9 collective-permute-start.1
  81.2 2.9 pack.7.refs_0_
  84.0 49.0 %all-to-all-done.1 = bf16[4,288,1152]{2,1,0:T(8,128)(2,1)} async-done(((bf16[4,288,1152]{2,1,0:T(8,128)(2,1)}), bf16[4,288,1152]{2,1,0:T(8,128)(2,1)}, u32[]{:S(2)}, u32[]{:S(2)}) %all-to-all-start.1) | async-done | bytes 2654240 | tf_op jit(solution)/shard_map/all_to_all | solution.py:285
  133.1 3.8 %all-to-all-start.2 = ((bf16[4,288,1152]{2,1,0:T(8,128)(2,1)}), bf16[4,288,1152]{2,1,0:T(8,128)(2,1)S(1)}, u32[]{:S(2)}, u32[]{:S(2)}) async-start(bf16[4,288,1152]{2,1,0:T(8,128)(2,1)} %gate.6.refs_6_), calls=%async_computation.2 | async-start | bytes 5308416 | tf_op jit(solution)/shard_map/all_to_all | solution.py:285
  138.7 2.1 pack.6.refs_0_
  140.9 2.8 slice.17
  143.7 4.5 %collective-permute-start.2 = (bf16[1152,768]{1,0:T(8,128)(2,1)}, bf16[1152,768]{1,0:T(8,128)(2,1)}, u32[]{:S(2)}, u32[]{:S(2)}) collective-permute-start(bf16[1152,768]{1,0:T(8,128)(2,1)} %slice.17), channel_id=1, source_target_pairs={{0,4},{4,8},{8,12},{12,16},{16,20},{20,24},{24,28},{1,5},{5,9},{9,... | collective-permute-start | bytes 5308424 | tf_op jit(solution)/shard_map/ppermute | solution.py:289
  148.1 1.9 collective-permute-start.3
  150.1 29.8 %attend.4 = (bf16[288,384]{1,0:T(8,128)(2,1)}, bf16[288,384]{1,0:T(8,128)(2,1)}, bf16[288,384]{1,0:T(8,128)(2,1)}, bf16[288,384]{1,0:T(8,128)(2,1)}) custom-call(s32[27]{0:T(128)} %reshape.58.refs_0_, bf16[1152,1152]{1,0:T(8,128)(2,1)} %bitcast.6, bf16[1152,768]{1,0:T(8,128)(2,1)} %collective-permute-done.refs_2_, ...), custom_call_target="tpu_custom_call" | custom-call | flops 24461180928 | bytes 7077888 | tf_op jit(solution)/shard_map/attend/pallas_call | solution.py:232
  179.9 1.7 collective-permute-start.10
  181.6 1.8 collective-permute-start.8
  183.9 22.1 %all-to-all-done.2.refs_0_ = bf16[4,288,1152]{2,1,0:T(8,128)(2,1)S(1)} async-done(((bf16[4,288,1152]{2,1,0:T(8,128)(2,1)}), bf16[4,288,1152]{2,1,0:T(8,128)(2,1)S(1)}, u32[]{:S(2)}, u32[]{:S(2)}) %all-to-all-start.2) | async-done | bytes 2654240 | tf_op jit(solution)/shard_map/all_to_all | solution.py:285
  207.5 1.6 slice.19
  209.1 3.5 %all-to-all-start.3 = ((bf16[4,288,384]{2,1,0:T(8,128)(2,1)}), bf16[4,288,384]{2,1,0:T(8,128)(2,1)S(1)}, u32[]{:S(2)}, u32[]{:S(2)}) async-start(bf16[4,288,384]{2,1,0:T(8,128)(2,1)} %gate.8.refs_6_), calls=%async_computation.3 | async-start | bytes 1769472 | tf_op jit(solution)/shard_map/all_to_all | solution.py:285
  212.7 5.6 %collective-permute-start.6 = (bf16[1152,768]{1,0:T(8,128)(2,1)S(1)}, bf16[1152,768]{1,0:T(8,128)(2,1)}, u32[]{:S(2)}, u32[]{:S(2)}) collective-permute-start(bf16[1152,768]{1,0:T(8,128)(2,1)S(1)} %slice.19), channel_id=1, source_target_pairs={{0,4},{4,8},{8,12},{12,16},{16,20},{20,24},{24,28},{1,5},{5,9},{9,... | collective-permute-start | bytes 5308424 | tf_op jit(solution)/shard_map/ppermute | solution.py:289
  218.3 1.9 collective-permute-start.7
  220.2 29.8 %attend.5 = (bf16[288,384]{1,0:T(8,128)(2,1)}, bf16[288,384]{1,0:T(8,128)(2,1)}, bf16[288,384]{1,0:T(8,128)(2,1)}, bf16[288,384]{1,0:T(8,128)(2,1)}) custom-call(s32[27]{0:T(128)} %reshape.58.refs_0_, bf16[1152,1152]{1,0:T(8,128)(2,1)} %bitcast.1.refs_3_.refs_1_.refs_5_, bf16[1152,768]{1,0:T(8,128)(2,1)} %collective-permute-done.2.refs_2_, ...), custom_call_target="tpu_custom_call" | custom-call | flops 24461180928 | bytes 7077888 | tf_op jit(solution)/shard_map/attend/pallas_call | solution.py:232
  252.1 3.6 %collective-permute-start.11 = (bf16[288,384]{1,0:T(8,128)(2,1)S(1)}, bf16[288,384]{1,0:T(8,128)(2,1)S(1)}, u32[]{:S(2)}, u32[]{:S(2)}) collective-permute-start(bf16[288,384]{1,0:T(8,128)(2,1)S(1)} %copy-done.23), channel_id=1, source_target_pairs={{0,3},{1,0},{2,1},{3,2},{4,7},{5,4},{6,5},{7,6},{8,11},{9,8},{10,9... | collective-permute-start | bytes 663560 | tf_op jit(solution)/shard_map/ppermute | solution.py:272
  256.4 1.9 collective-permute-start.4
  258.3 2.6 collective-permute-start.5
  260.9 29.7 %attend.6 = (bf16[288,384]{1,0:T(8,128)(2,1)}, bf16[288,384]{1,0:T(8,128)(2,1)}, bf16[288,384]{1,0:T(8,128)(2,1)}, bf16[288,384]{1,0:T(8,128)(2,1)}) custom-call(s32[27]{0:T(128)} %reshape.58.refs_0_, bf16[1152,1152]{1,0:T(8,128)(2,1)} %bitcast.11, bf16[1152,768]{1,0:T(8,128)(2,1)} %collective-permute-done.6.refs_2_, ...), custom_call_target="tpu_custom_call" | custom-call | flops 24461180928 | bytes 7077888 | tf_op jit(solution)/shard_map/attend/pallas_call | solution.py:232
  290.7 3.1 collective-permute-start.17
  295.3 18.3 %attend.7 = (bf16[288,128]{1,0:T(8,128)(2,1)}, bf16[288,128]{1,0:T(8,128)(2,1)}, bf16[288,128]{1,0:T(8,128)(2,1)}, bf16[288,128]{1,0:T(8,128)(2,1)}) custom-call(s32[27]{0:T(128)} %reshape.58.refs_0_, bf16[1152,384]{1,0:T(8,128)(2,1)} %bitcast.14, bf16[1152,256]{1,0:T(8,128)(2,1)} %copy-done.19, bf16[1152,256]{1,0:T(8,128)(2,1)} %copy-done.20, ...), custom_call_target="tpu_custom_call" | custom-call | flops 8153726976 | bytes 2359296 | tf_op jit(solution)/shard_map/attend/pallas_call | solution.py:232
  313.7 3.0 collective-permute-start.14
  318.4 2.7 place.2.refs_4_
  322.8 1.7 place.3
  (88 shorter events, 14.4 us)
Async XLA Ops:
  2.8 64.2 %all-to-all-start = ((bf16[4,288,1152]{2,1,0:T(8,128)(2,1)}), bf16[4,288,1152]{2,1,0:T(8,128)(2,1)S(1)}, u32[]{:S(2)}, u32[]{:S(2)}) async-start(bf16[4,288,1152]{2,1,0:T(8,128)(2,1)} %pack.5), calls=%async_computation | async-start | bytes 5308416 | tf_op jit(solution)/shard_map/all_to_all | solution.py:285
  68.6 4.9 %copy-start.1 = (bf16[4,288,1152]{2,1,0:T(8,128)(2,1)S(1)}, bf16[4,288,1152]{2,1,0:T(8,128)(2,1)}, u32[]{:S(2)}) copy-start(bf16[4,288,1152]{2,1,0:T(8,128)(2,1)} %copy-done) | copy-start | bytes 7962628
  68.6 64.5 %all-to-all-start.1 = ((bf16[4,288,1152]{2,1,0:T(8,128)(2,1)}), bf16[4,288,1152]{2,1,0:T(8,128)(2,1)}, u32[]{:S(2)}, u32[]{:S(2)}) async-start(bf16[4,288,1152]{2,1,0:T(8,128)(2,1)} %gate.5), calls=%async_computation.1 | async-start | bytes 5308416 | tf_op jit(solution)/shard_map/all_to_all | solution.py:285
  74.8 75.3 %collective-permute-start = (bf16[1152,768]{1,0:T(8,128)(2,1)}, bf16[1152,768]{1,0:T(8,128)(2,1)}, u32[]{:S(2)}, u32[]{:S(2)}) collective-permute-start(bf16[1152,768]{1,0:T(8,128)(2,1)} %slice.16), channel_id=1, source_target_pairs={{0,4},{4,8},{8,12},{12,16},{16,20},{20,24},{24,28},{1,5},{5,9},{9,... | collective-permute-start | bytes 5308424 | tf_op jit(solution)/shard_map/ppermute | solution.py:289
  79.3 70.8 %collective-permute-start.1 = (bf16[1152,768]{1,0:T(8,128)(2,1)}, bf16[1152,768]{1,0:T(8,128)(2,1)}, u32[]{:S(2)}, u32[]{:S(2)}) collective-permute-start(bf16[1152,768]{1,0:T(8,128)(2,1)} %slice.16), channel_id=1, source_target_pairs={{4,0},{8,4},{12,8},{16,12},{20,16},{24,20},{28,24},{5,1},{9,5},{13... | collective-permute-start | bytes 5308424 | tf_op jit(solution)/shard_map/ppermute | solution.py:289
  133.1 3.9 %copy-start.18 = (s32[3]{0:T(128)S(1)}, s32[3]{0:T(128)}, u32[]{:S(2)}) copy-start(s32[3]{0:T(128)} %param.9) | copy-start | bytes 40
  133.1 4.5 %copy-start.13 = (s32[1152,10]{0,1:T(8,128)S(1)}, s32[1152,10]{0,1:T(8,128)}, u32[]{:S(2)}) copy-start(s32[1152,10]{0,1:T(8,128)} %param.11) | copy-start | bytes 138244
  133.1 72.9 %all-to-all-start.2 = ((bf16[4,288,1152]{2,1,0:T(8,128)(2,1)}), bf16[4,288,1152]{2,1,0:T(8,128)(2,1)S(1)}, u32[]{:S(2)}, u32[]{:S(2)}) async-start(bf16[4,288,1152]{2,1,0:T(8,128)(2,1)} %gate.6.refs_6_), calls=%async_computation.2 | async-start | bytes 5308416 | tf_op jit(solution)/shard_map/all_to_all | solution.py:285
  143.7 69.0 %collective-permute-start.2 = (bf16[1152,768]{1,0:T(8,128)(2,1)}, bf16[1152,768]{1,0:T(8,128)(2,1)}, u32[]{:S(2)}, u32[]{:S(2)}) collective-permute-start(bf16[1152,768]{1,0:T(8,128)(2,1)} %slice.17), channel_id=1, source_target_pairs={{0,4},{4,8},{8,12},{12,16},{16,20},{20,24},{24,28},{1,5},{5,9},{9,... | collective-permute-start | bytes 5308424 | tf_op jit(solution)/shard_map/ppermute | solution.py:289
  148.1 70.1 %collective-permute-start.3 = (bf16[1152,768]{1,0:T(8,128)(2,1)}, bf16[1152,768]{1,0:T(8,128)(2,1)}, u32[]{:S(2)}, u32[]{:S(2)}) collective-permute-start(bf16[1152,768]{1,0:T(8,128)(2,1)} %slice.17), channel_id=1, source_target_pairs={{4,0},{8,4},{12,8},{16,12},{20,16},{24,20},{28,24},{5,1},{9,5},{13... | collective-permute-start | bytes 5308424 | tf_op jit(solution)/shard_map/ppermute | solution.py:289
  179.9 72.2 %collective-permute-start.10 = (bf16[288,384]{1,0:T(8,128)(2,1)}, bf16[288,384]{1,0:T(8,128)(2,1)S(1)}, u32[]{:S(2)}, u32[]{:S(2)}) collective-permute-start(bf16[288,384]{1,0:T(8,128)(2,1)} %get-tuple-element.25), channel_id=1, source_target_pairs={{0,1},{1,2},{2,3},{3,0},{4,5},{5,6},{6,7},{7,4},{8,9},{9,10},{10,1... | collective-permute-start | bytes 663560 | tf_op jit(solution)/shard_map/ppermute | solution.py:272
  181.6 74.1 %collective-permute-start.8 = (bf16[288,384]{1,0:T(8,128)(2,1)}, bf16[288,384]{1,0:T(8,128)(2,1)S(1)}, u32[]{:S(2)}, u32[]{:S(2)}) collective-permute-start(bf16[288,384]{1,0:T(8,128)(2,1)} %get-tuple-element.23), channel_id=1, source_target_pairs={{0,3},{1,0},{2,1},{3,2},{4,7},{5,4},{6,5},{7,6},{8,11},{9,8},{10,9... | collective-permute-start | bytes 663560 | tf_op jit(solution)/shard_map/ppermute | solution.py:272
  183.4 72.4 %collective-permute-start.9 = (bf16[288,384]{1,0:T(8,128)(2,1)}, bf16[288,384]{1,0:T(8,128)(2,1)S(1)}, u32[]{:S(2)}, u32[]{:S(2)}) collective-permute-start(bf16[288,384]{1,0:T(8,128)(2,1)} %get-tuple-element.24), channel_id=1, source_target_pairs={{0,2},{1,3},{2,0},{3,1},{4,6},{5,7},{6,4},{7,5},{8,10},{9,11},{10,... | collective-permute-start | bytes 663560 | tf_op jit(solution)/shard_map/ppermute | solution.py:272
  209.1 40.9 %all-to-all-start.3 = ((bf16[4,288,384]{2,1,0:T(8,128)(2,1)}), bf16[4,288,384]{2,1,0:T(8,128)(2,1)S(1)}, u32[]{:S(2)}, u32[]{:S(2)}) async-start(bf16[4,288,384]{2,1,0:T(8,128)(2,1)} %gate.8.refs_6_), calls=%async_computation.3 | async-start | bytes 1769472 | tf_op jit(solution)/shard_map/all_to_all | solution.py:285
  212.7 43.7 %collective-permute-start.6 = (bf16[1152,768]{1,0:T(8,128)(2,1)S(1)}, bf16[1152,768]{1,0:T(8,128)(2,1)}, u32[]{:S(2)}, u32[]{:S(2)}) collective-permute-start(bf16[1152,768]{1,0:T(8,128)(2,1)S(1)} %slice.19), channel_id=1, source_target_pairs={{0,4},{4,8},{8,12},{12,16},{16,20},{20,24},{24,28},{1,5},{5,9},{9,... | collective-permute-start | bytes 5308424 | tf_op jit(solution)/shard_map/ppermute | solution.py:289
  218.3 40.0 %collective-permute-start.7 = (bf16[1152,768]{1,0:T(8,128)(2,1)S(1)}, bf16[1152,768]{1,0:T(8,128)(2,1)}, u32[]{:S(2)}, u32[]{:S(2)}) collective-permute-start(bf16[1152,768]{1,0:T(8,128)(2,1)S(1)} %slice.19), channel_id=1, source_target_pairs={{4,0},{8,4},{12,8},{16,12},{20,16},{24,20},{28,24},{5,1},{9,5},{13... | collective-permute-start | bytes 5308424 | tf_op jit(solution)/shard_map/ppermute | solution.py:289
  250.0 5.8 %copy-start.21 = (bf16[288,384]{1,0:T(8,128)(2,1)S(1)}, bf16[288,384]{1,0:T(8,128)(2,1)}, u32[]{:S(2)}) copy-start(bf16[288,384]{1,0:T(8,128)(2,1)} %get-tuple-element.29) | copy-start | bytes 663556
  250.0 5.7 %copy-start.22 = (bf16[288,384]{1,0:T(8,128)(2,1)S(1)}, bf16[288,384]{1,0:T(8,128)(2,1)}, u32[]{:S(2)}) copy-start(bf16[288,384]{1,0:T(8,128)(2,1)} %get-tuple-element.28) | copy-start | bytes 663556
  252.1 8.8 %copy-start.4 = (bf16[288,384]{1,0:T(8,128)(2,1)}, bf16[288,384]{1,0:T(8,128)(2,1)S(1)}, u32[]{:S(2)}) copy-start(bf16[288,384]{1,0:T(8,128)(2,1)S(1)} %collective-permute-done.10.refs_9_.refs_3_) | copy-start | bytes 663556
  252.1 38.6 %collective-permute-start.11 = (bf16[288,384]{1,0:T(8,128)(2,1)S(1)}, bf16[288,384]{1,0:T(8,128)(2,1)S(1)}, u32[]{:S(2)}, u32[]{:S(2)}) collective-permute-start(bf16[288,384]{1,0:T(8,128)(2,1)S(1)} %copy-done.23), channel_id=1, source_target_pairs={{0,3},{1,0},{2,1},{3,2},{4,7},{5,4},{6,5},{7,6},{8,11},{9,8},{10,9... | collective-permute-start | bytes 663560 | tf_op jit(solution)/shard_map/ppermute | solution.py:272
  255.7 5.2 %copy-start.5 = (bf16[288,384]{1,0:T(8,128)(2,1)}, bf16[288,384]{1,0:T(8,128)(2,1)S(1)}, u32[]{:S(2)}) copy-start(bf16[288,384]{1,0:T(8,128)(2,1)S(1)} %collective-permute-done.8.refs_7_.refs_1_) | copy-start | bytes 663556
  255.7 38.0 %collective-permute-start.12 = (bf16[288,384]{1,0:T(8,128)(2,1)S(1)}, bf16[288,384]{1,0:T(8,128)(2,1)S(1)}, u32[]{:S(2)}, u32[]{:S(2)}) collective-permute-start(bf16[288,384]{1,0:T(8,128)(2,1)S(1)} %copy-done.22), channel_id=1, source_target_pairs={{0,2},{1,3},{2,0},{3,1},{4,6},{5,7},{6,4},{7,5},{8,10},{9,11},{10,... | collective-permute-start | bytes 663560 | tf_op jit(solution)/shard_map/ppermute | solution.py:272
  255.8 5.1 %copy-start.6 = (bf16[288,384]{1,0:T(8,128)(2,1)}, bf16[288,384]{1,0:T(8,128)(2,1)S(1)}, u32[]{:S(2)}) copy-start(bf16[288,384]{1,0:T(8,128)(2,1)S(1)} %collective-permute-done.9.refs_8_.refs_2_) | copy-start | bytes 663556
  255.8 38.2 %collective-permute-start.13 = (bf16[288,384]{1,0:T(8,128)(2,1)S(1)}, bf16[288,384]{1,0:T(8,128)(2,1)S(1)}, u32[]{:S(2)}, u32[]{:S(2)}) collective-permute-start(bf16[288,384]{1,0:T(8,128)(2,1)S(1)} %copy-done.21), channel_id=1, source_target_pairs={{0,1},{1,2},{2,3},{3,0},{4,5},{5,6},{6,7},{7,4},{8,9},{9,10},{10,1... | collective-permute-start | bytes 663560 | tf_op jit(solution)/shard_map/ppermute | solution.py:272
  256.4 37.9 %collective-permute-start.4 = (bf16[1152,256]{1,0:T(8,128)(2,1)S(1)}, bf16[1152,256]{1,0:T(8,128)(2,1)S(1)}, u32[]{:S(2)}, u32[]{:S(2)}) collective-permute-start(bf16[1152,256]{1,0:T(8,128)(2,1)S(1)} %slice.18), channel_id=1, source_target_pairs={{0,4},{4,8},{8,12},{12,16},{16,20},{20,24},{24,28},{1,5},{5,9},{9,... | collective-permute-start | bytes 1769480 | tf_op jit(solution)/shard_map/ppermute | solution.py:289
  258.3 36.0 %collective-permute-start.5 = (bf16[1152,256]{1,0:T(8,128)(2,1)S(1)}, bf16[1152,256]{1,0:T(8,128)(2,1)S(1)}, u32[]{:S(2)}, u32[]{:S(2)}) collective-permute-start(bf16[1152,256]{1,0:T(8,128)(2,1)S(1)} %slice.18), channel_id=1, source_target_pairs={{4,0},{8,4},{12,8},{16,12},{20,16},{24,20},{28,24},{5,1},{9,5},{13... | collective-permute-start | bytes 1769480 | tf_op jit(solution)/shard_map/ppermute | solution.py:289
  290.7 26.3 %collective-permute-start.17 = (bf16[288,384]{1,0:T(8,128)(2,1)}, bf16[288,384]{1,0:T(8,128)(2,1)S(1)}, u32[]{:S(2)}, u32[]{:S(2)}) collective-permute-start(bf16[288,384]{1,0:T(8,128)(2,1)} %get-tuple-element.34), channel_id=1, source_target_pairs={{0,3},{1,0},{2,1},{3,2},{4,7},{5,4},{6,5},{7,6},{8,11},{9,8},{10,9... | collective-permute-start | bytes 663560 | tf_op jit(solution)/shard_map/ppermute | solution.py:272
  293.7 23.3 %collective-permute-start.18 = (bf16[288,384]{1,0:T(8,128)(2,1)}, bf16[288,384]{1,0:T(8,128)(2,1)S(1)}, u32[]{:S(2)}, u32[]{:S(2)}) collective-permute-start(bf16[288,384]{1,0:T(8,128)(2,1)} %get-tuple-element.35), channel_id=1, source_target_pairs={{0,2},{1,3},{2,0},{3,1},{4,6},{5,7},{6,4},{7,5},{8,10},{9,11},{10,... | collective-permute-start | bytes 663560 | tf_op jit(solution)/shard_map/ppermute | solution.py:272
  294.0 23.0 %collective-permute-start.19 = (bf16[288,384]{1,0:T(8,128)(2,1)}, bf16[288,384]{1,0:T(8,128)(2,1)S(1)}, u32[]{:S(2)}, u32[]{:S(2)}) collective-permute-start(bf16[288,384]{1,0:T(8,128)(2,1)} %get-tuple-element.36), channel_id=1, source_target_pairs={{0,1},{1,2},{2,3},{3,0},{4,5},{5,6},{6,7},{7,4},{8,9},{9,10},{10,1... | collective-permute-start | bytes 663560 | tf_op jit(solution)/shard_map/ppermute | solution.py:272
  313.7 7.5 %collective-permute-start.14 = (bf16[288,128]{1,0:T(8,128)(2,1)}, bf16[288,128]{1,0:T(8,128)(2,1)S(1)}, u32[]{:S(2)}, u32[]{:S(2)}) collective-permute-start(bf16[288,128]{1,0:T(8,128)(2,1)} %get-tuple-element.31), channel_id=1, source_target_pairs={{0,3},{1,0},{2,1},{3,2},{4,7},{5,4},{6,5},{7,6},{8,11},{9,8},{10,9... | collective-permute-start | bytes 221192 | tf_op jit(solution)/shard_map/ppermute | solution.py:272
  316.6 4.6 %collective-permute-start.15 = (bf16[288,128]{1,0:T(8,128)(2,1)}, bf16[288,128]{1,0:T(8,128)(2,1)S(1)}, u32[]{:S(2)}, u32[]{:S(2)}) collective-permute-start(bf16[288,128]{1,0:T(8,128)(2,1)} %get-tuple-element.32), channel_id=1, source_target_pairs={{0,2},{1,3},{2,0},{3,1},{4,6},{5,7},{6,4},{7,5},{8,10},{9,11},{10,... | collective-permute-start | bytes 221192 | tf_op jit(solution)/shard_map/ppermute | solution.py:272
  316.9 5.2 %collective-permute-start.16 = (bf16[288,128]{1,0:T(8,128)(2,1)}, bf16[288,128]{1,0:T(8,128)(2,1)S(1)}, u32[]{:S(2)}, u32[]{:S(2)}) collective-permute-start(bf16[288,128]{1,0:T(8,128)(2,1)} %get-tuple-element.33), channel_id=1, source_target_pairs={{0,1},{1,2},{2,3},{3,0},{4,5},{5,6},{6,7},{7,4},{8,9},{9,10},{10,1... | collective-permute-start | bytes 221192 | tf_op jit(solution)/shard_map/ppermute | solution.py:272
  (16 other events, 21.5 us)
